TPU v7x, 128 devices: a whole 4x4x4 slice. The times are simulated.
128 devices in a mesh: dp: 4 (over x), pipe: 2 (over core), tensor: 16 (over z, y).
Axes of the slice: x: 4, y: 4, z: 4, core: 2. Of those that a mesh axis runs over, the one named last changes fastest.
Arguments:
- queries: bfloat16 [8, 34, 16384], P(('dp', 'pipe')), parts along dimension 0, may hold values from -80 to 80
- cache_k: bfloat16 [8, 3, 32768, 1024], P(('dp', 'pipe'), None, 'tensor'), parts along dimension 0, may hold values from -4 to 4
- cache_v: bfloat16 [8, 3, 32768, 1024], P(('dp', 'pipe'), None, 'tensor'), parts along dimension 0, may hold values from -6 to 6
- dec_lengths: int32 [8, 2], P(('dp', 'pipe')), parts along dimension 0, may hold values from 2 to 32768, as said below
- pre_starts: int32 [8], P(('dp', 'pipe')), parts along dimension 0, may hold values from 0 to 32736, as said below
Outputs:
- handed: bfloat16 [8, 34, 16384], P(('dp', 'pipe'), None, 'tensor'), parts along dimension 0
There are 4 independent parts, one for each index of `dp`. A program takes and returns all parts, laid end to end along the dimension named above; each array names one. Nothing has to cross between parts.
Inputs may be any that keep to these rules, and one draw needn't show every extreme that they name: `dec_lengths`: every decode row has at least two live positions; some row of some section uses all 32768 positions. `pre_starts`: every prefill block fits in the cache; some section's block ends at the last position.
All inputs are finite; a program needn't handle non-finite values.
Results may differ from a plain program's by a relative error of at most 0.0075.
Values may be sent and summed in bfloat16 or wider, within the bound.
No kernel may reach another device: no remote copies, remote signals or barrier semaphores. Data moves between devices by JAX's collectives and lax.ppermute only.
A program may use at most 192 MiB of HBM per device.

v0:
```python
import math

import jax
import jax.numpy as jnp
from jax import lax
from jax.sharding import PartitionSpec as P

HQ = 128
KVH = 8
HD = 128


NEGATIVE_FILL = -1e30


def joined(part, axis, combine):
    gathered = jax.tree.map(lambda a: lax.all_gather(a, axis), part)

    def take(source):
        return jax.tree.map(lambda a: lax.dynamic_index_in_dim(a, source, 0, False), gathered)

    return lax.fori_loop(
        1, lax.axis_size(axis), lambda source, state: combine(state, take(source)), take(0)
    )


def from_behind(value, axis, steps):
    count = lax.axis_size(axis)
    pairs = [(source, (source + steps) % count) for source in range(count)]
    return lax.ppermute(value, axis, pairs)


def partial_softmax(scores, live):
    maxima = jnp.max(jnp.where(live, scores, NEGATIVE_FILL), axis=-1)
    weights = jnp.where(live, jnp.exp(scores - maxima[..., None]), 0.0)
    return (weights.astype(jnp.bfloat16), maxima, jnp.sum(weights, axis=-1))


def combine(first, second):
    maxima = jnp.maximum(first[1], second[1])
    factor_first = jnp.exp(first[1] - maxima)
    factor_second = jnp.exp(second[1] - maxima)
    weighted = first[0] * factor_first[..., None] + second[0] * factor_second[..., None]
    totals = first[2] * factor_first + second[2] * factor_second
    return (weighted, maxima, totals)


def on_device(queries, cache_k, cache_v, dec_lengths, pre_starts):
    query_rows = queries[0]
    key_cache = cache_k[0]
    value_cache = cache_v[0]
    dec_rows = key_cache.shape[0] - 1
    pre_rows = query_rows.shape[0] - dec_rows
    local_len = key_cache.shape[1]
    group_size = HQ // KVH
    softmax_scale = 1.0 / math.sqrt(HD)
    offset = lax.axis_index("tensor") * local_len
    positions = offset + jnp.arange(local_len, dtype=jnp.int32)
    dec_query = query_rows[:dec_rows].reshape(dec_rows, KVH, group_size, HD)
    dec_keys = key_cache[:dec_rows].reshape(dec_rows, local_len, KVH, HD)
    dec_values = value_cache[:dec_rows].reshape(dec_rows, local_len, KVH, HD)
    dec_scores = (
        jnp.einsum("bkgd,bpkd->bkgp", dec_query, dec_keys, preferred_element_type=jnp.float32)
        * softmax_scale
    )
    live_dec = (positions[None, :] < dec_lengths[0][:, None])[:, None, None, :]
    dec_weights, dec_maxima, dec_totals = partial_softmax(dec_scores, live_dec)
    dec_weighted = jnp.einsum(
        "bkgp,bpkd->bkgd", dec_weights, dec_values, preferred_element_type=jnp.float32
    )
    span_start = pre_starts[0]
    token_index = jnp.arange(pre_rows, dtype=jnp.int32)
    pre_query = query_rows[dec_rows:].reshape(pre_rows, KVH, group_size, HD)
    pre_keys = key_cache[dec_rows].reshape(local_len, KVH, HD)
    pre_values = value_cache[dec_rows].reshape(local_len, KVH, HD)
    pre_scores = (
        jnp.einsum("qkgd,pkd->qkgp", pre_query, pre_keys, preferred_element_type=jnp.float32)
        * softmax_scale
    )
    live_pre = (positions[None, :] <= span_start + token_index[:, None])[:, None, None, :]
    pre_weights, pre_maxima, pre_totals = partial_softmax(pre_scores, live_pre)
    pre_weighted = jnp.einsum(
        "qkgp,pkd->qkgd", pre_weights, pre_values, preferred_element_type=jnp.float32
    )
    weighted = jnp.concatenate(
        [dec_weighted.reshape(dec_rows, HQ, HD), pre_weighted.reshape(pre_rows, HQ, HD)], 0
    )
    maxima = jnp.concatenate(
        [dec_maxima.reshape(dec_rows, HQ), pre_maxima.reshape(pre_rows, HQ)], 0
    )
    totals = jnp.concatenate(
        [dec_totals.reshape(dec_rows, HQ), pre_totals.reshape(pre_rows, HQ)], 0
    )
    row_count = weighted.shape[0]
    weighted, maxima, totals = joined((weighted, maxima, totals), "tensor", combine)
    head_share = HQ // lax.axis_size("tensor")
    start_head = lax.axis_index("tensor") * head_share
    picked = lax.dynamic_slice_in_dim(weighted, start_head, head_share, 1)
    picked_totals = lax.dynamic_slice_in_dim(totals, start_head, head_share, 1)
    own_share = (
        (picked / picked_totals[..., None]).astype(jnp.bfloat16).reshape(row_count, head_share * HD)
    )
    handed = from_behind(own_share, "pipe", 1)
    return handed[None]


def solution(mesh):
    in_specs = (
        P(("dp", "pipe"), None, None),
        P(("dp", "pipe"), None, "tensor", None),
        P(("dp", "pipe"), None, "tensor", None),
        P(("dp", "pipe"), None),
        P(("dp", "pipe")),
    )
    out_specs = P(("dp", "pipe"), None, "tensor")
    return jax.shard_map(
        on_device, mesh=mesh, in_specs=in_specs, out_specs=out_specs, check_vma=False
    )
```

profile of v0, /device:TPU:1, one launch (start us, length us, event | category | flops | bytes accessed | tf_op | source)
XLA Modules:
  0.0 381.1 jit_solution(18062053848322736280)
XLA Ops:
  9.1 4.6 %slice.30 = bf16[1,1,2048,1024]{3,2,1,0:T(8,128)(2,1)} slice(bf16[1,3,2048,1024]{3,2,1,0:T(8,128)(2,1)} %param.8), slice={[0:1], [2:3], [0:2048], [0:1024]} | slice | bytes 8388608 | tf_op jit(solution)/shard_map/slice | solution.py:74
  13.7 7.6 %slice.28 = bf16[1,2,2048,1024]{3,2,1,0:T(8,128)(2,1)} slice(bf16[1,3,2048,1024]{3,2,1,0:T(8,128)(2,1)} %param.8), slice={[0:1], [0:2], [0:2048], [0:1024]} | slice | bytes 16777216 | tf_op jit(solution)/shard_map/slice | solution.py:60
  21.3 4.6 %slice.32 = bf16[1,1,2048,1024]{3,2,1,0:T(8,128)(2,1)} slice(bf16[1,3,2048,1024]{3,2,1,0:T(8,128)(2,1)} %param.9), slice={[0:1], [2:3], [0:2048], [0:1024]} | slice | bytes 8388608 | tf_op jit(solution)/shard_map/slice | solution.py:75
  25.9 7.6 %slice.29 = bf16[1,2,2048,1024]{3,2,1,0:T(8,128)(2,1)} slice(bf16[1,3,2048,1024]{3,2,1,0:T(8,128)(2,1)} %param.9), slice={[0:1], [0:2], [0:2048], [0:1024]} | slice | bytes 16777216 | tf_op jit(solution)/shard_map/slice | solution.py:61
  34.6 6.5 %copy.46 = bf16[1,1,2048,1024]{2,3,1,0:T(8,128)(2,1)} copy(bf16[1,1,2048,1024]{3,2,1,0:T(8,128)(2,1)} %slice.30) | data formatting | bytes 8388608
  41.1 6.5 %copy.47 = bf16[1,1,2048,1024]{2,3,1,0:T(8,128)(2,1)} copy(bf16[1,1,2048,1024]{3,2,1,0:T(8,128)(2,1)} %slice.32) | data formatting | bytes 8388608
  47.6 11.6 %copy.44 = bf16[1,2,2048,1024]{2,3,1,0:T(8,128)(2,1)} copy(bf16[1,2,2048,1024]{3,2,1,0:T(8,128)(2,1)} %slice.28) | data formatting | bytes 16777216
  59.2 11.7 %copy.45 = bf16[1,2,2048,1024]{2,3,1,0:T(8,128)(2,1)} copy(bf16[1,2,2048,1024]{3,2,1,0:T(8,128)(2,1)} %slice.29) | data formatting | bytes 16777216
  70.9 16.4 %fusion.3 = (f32[32,8,16]{0,2,1:T(8,128)S(1)}, f32[8,2048,32,16]{1,2,3,0:T(8,128)}) fusion(pred[32,2048]{1,0:T(8,128)(4,1)S(1)} %broadcast_compare_fusion, bf16[2048,8,128,1]{0,2,3,1:T(8,128)(2,1)} %bitcast.88, bf16[32,8,16,128]{3,2,1,0:T(8,128)(2,1)S(1)} %bitcast.90), kind=kOutput, calls=%fused_computation.10 | convolution fusion | flops 2172645376 | bytes 38879232 | tf_op jit(solution)/shard_map/qkgd,pkd->qkgp/dot_general | solution.py:77
  87.3 14.8 %fusion.13 = f32[32,8,16,128]{3,0,2,1:T(8,128)S(1)} fusion(bf16[2048,8,128,1]{0,2,3,1:T(8,128)(2,1)} %bitcast.92, f32[8,2048,32,16]{1,2,3,0:T(8,128)} %get-tuple-element.210, f32[32,8,16]{0,2,1:T(8,128)S(1)} %get-tuple-element.209, pred[32,2048]{1,0:T(8,128)(4,1)S(1)} %broadcast_compare_fusion), kind=kOutput, calls=%fused_computation.23 | convolution fusion | flops 2181038080 | bytes 39927808 | tf_op jit(solution)/shard_map/qkgp,pkd->qkgd/dot_general | solution.py:82
  103.4 4.8 %select_reduce_fusion = (f32[2,8,16]{2,1,0:T(8,128)S(1)}, f32[2,8,16,2048]{3,2,1,0:T(8,128)S(1)}) fusion(pred[2,2048]{1,0:T(4,128)(4,1)S(1)} %broadcast_compare_fusion.1, bf16[2,8,16,128]{3,2,1,0:T(8,128)(2,1)S(1)} %bitcast.95, bf16[2,2048,8,128]{1,3,2,0:T(8,128)(2,1)} %bitcast.84), kind=kOutput, calls=%fused_computation.20 | convolution fusion | flops 135790336 | bytes 10556416 | tf_op jit(solution)/shard_map/bkgd,bpkd->bkgp/dot_general | solution.py:63
  108.2 2.3 fusion.16
  112.8 15.7 %fusion.6 = f32[32,8,16]{0,2,1:T(8,128)S(1)} fusion(f32[8,2048,32,16]{1,2,3,0:T(8,128)} %get-tuple-element.210, f32[32,8,16]{0,2,1:T(8,128)S(1)} %get-tuple-element.209, pred[32,2048]{1,0:T(8,128)(4,1)S(1)} %broadcast_compare_fusion), kind=kLoop, calls=%fused_computation.13 | loop fusion | flops 33550336 | bytes 33652736 | tf_op jit(solution)/shard_map/reduce_sum | solution.py:36
  128.7 24.1 %all-gather.4 = f32[16,34,128]{2,1,0:T(8,128)S(1)} all-gather(f32[1,34,128]{2,1,0:T(8,128)S(1)} %maximum_bitcast_fusion.1), channel_id=4, replica_groups=mesh['dp'=4,'pipe'=2,'tensor'=16] {'tensor'}, dimensions={0}, use_global_device_ids=true | all-gather | bytes 295936 | tf_op jit(solution)/shard_map/all_gather | solution.py:17
  152.8 20.2 %all-gather.3 = f32[16,34,128]{2,1,0:T(8,128)S(1)} all-gather(f32[1,34,128]{2,1,0:T(8,128)S(1)} %maximum_bitcast_fusion), channel_id=3, replica_groups=mesh['dp'=4,'pipe'=2,'tensor'=16] {'tensor'}, dimensions={0}, use_global_device_ids=true | all-gather | bytes 295936 | tf_op jit(solution)/shard_map/all_gather | solution.py:17
  173.0 153.3 %all-gather.7.cloned.1.call-done = f32[544,128,128]{2,1,0:T(8,128)} async-done(((f32[34,128,128]{2,1,0:T(8,128)}), f32[544,128,128]{2,1,0:T(8,128)}) %all-gather.7.cloned.1.call-update) | async-done | bytes 35651600 | tf_op jit(solution)/shard_map/all_gather | solution.py:17
  328.1 43.6 %while.19 = (s32[]{:T(128)}, f32[34,128,128]{2,1,0:T(8,128)S(1)}, f32[34,128]{1,0:T(8,128)S(1)}, f32[34,128]{1,0:T(8,128)S(1)}, f32[16,34,128]{2,1,0:T(8,128)S(1...) while((s32[]{:T(128)}, f32[34,128,128]{2,1,0:T(8,128)S(1)}, ...), condition=%wide.region_5.6_spmd, body=%wide.region_4.5_spmd.sunk | while | flops 1697285 | bytes 6858895 | solution.py:22
  328.1 2.8 fusion.35
  331.1 2.8 fusion.35
  334.0 2.8 fusion.35
  336.9 2.8 fusion.35
  339.8 2.8 fusion.35
  342.7 2.8 fusion.35
  345.6 2.8 fusion.35
  348.5 2.8 fusion.35
  351.4 2.8 fusion.35
  354.3 2.8 fusion.35
  357.2 2.8 fusion.35
  360.1 2.8 fusion.35
  363.0 2.8 fusion.35
  365.9 2.8 fusion.35
  368.8 2.8 fusion.35
  (51 shorter events, 11.4 us)
Async XLA Ops:
  6.5 319.8 %all-gather.7.cloned.1.call-start = ((), (), s32[]{:S(2)}) async-start(), calls=%async_computation | async-start | bytes 37879808 | tf_op jit(solution)/shard_map/all_gather | solution.py:17
  25.9 8.3 %copy-start = (s32[1,2]{1,0:T(1,128)S(1)}, s32[1,2]{1,0:T(1,128)}, u32[]{:S(2)}) copy-start(s32[1,2]{1,0:T(1,128)} %param.10) | copy-start | bytes 28
  102.1 6.1 %slice-start = ((s8[8388608]{0:T(1024)(128)(4,1)}), s8[4194304]{0:T(1024)(128)(4,1)S(1)}, s32[]{:S(2)}) async-start(s8[8388608]{0:T(1024)(128)(4,1)} %bitcast.85), calls=%async_computation.1 | async-start | bytes 8388608
  103.4 4.8 %slice-start.1 = ((s8[8388608]{0:T(1024)(128)(4,1)}), s8[4194304]{0:T(1024)(128)(4,1)S(1)}, s32[]{:S(2)}) async-start(s8[8388608]{0:T(1024)(128)(4,1)} %bitcast.85), calls=%async_computation.2 | async-start | bytes 8388608
  371.9 1.7 collective-permute-start
Sparse Core Ops, SparseCore 0:
  112.2 214.0 all-gather.6
where the time goes:
time: 383 us; the launch traced here: 381 us
  waiting for transfers between devices  154 us (40%)
  local copies, waits for them, and re-layouts  67.5 us (18%)
  other arithmetic  61.2 us (16%)
  blocking collectives  44.4 us (12%)
  matrix products  38.3 us (10%)
  between operations  14.2 us (4%)
    all_gather x1, waiting for transfers between devices, joined(): gathered = jax.tree.map(lambda a: lax.all_gather(a, axis), part)  153 us
    all_gather x2, blocking collectives, joined(): gathered = jax.tree.map(lambda a: lax.all_gather(a, axis), part)  44.4 us
    add x15, other arithmetic, combine(): first[0] * factor_first[..., None] + second[0] * factor_second[..., None]  42.7 us
    unnamed x17, local copies, waits for them, and re-layouts  39.9 us
    dot_general x1, matrix products, on_device(): jnp.einsum('qkgd,pkd->qkgp', pre_query, pre_keys, preferred_element_type=...  16.4 us
    reduce_sum x2, other arithmetic, partial_softmax(): return (weights.astype(jnp.bfloat16), maxima, jnp.sum(weights, axis=-1))  16.2 us
    dot_general x1, matrix products, on_device(): jnp.einsum('qkgp,pkd->qkgd', pre_weights, pre_values, preferred_element_t...  14.8 us
  transfers between devices with their start and end apart: 2, of which 2 were waited for; matrix products, arithmetic and copies ran while one was open for 4% of the time, Pallas kernels for 0%

commit v1 on v0

v1 whole, which is shorter than its diff:
```python
import math

import jax
import jax.numpy as jnp
from jax import lax
from jax.experimental import pallas as pl
from jax.experimental.pallas import tpu as pltpu
from jax.sharding import PartitionSpec as P

HQ = 128
KVH = 8
HD = 128
GROUP = HQ // KVH
HALF = GROUP // 2
DEC = 2
PRE = 32
LANES = GROUP * PRE
TILE = 512
ROWS = 160
SCALE = math.log2(math.e) / math.sqrt(HD)
DEAD = -1e30
FLOOR = -1e29


def three_parts(x):
    first = x.astype(jnp.bfloat16).astype(jnp.float32)
    rest = x - first
    second = rest.astype(jnp.bfloat16).astype(jnp.float32)
    return first, second, rest - second


def nt_dot(a, b):
    return lax.dot_general(a, b, (((1,), (1,)), ((), ())), preferred_element_type=jnp.float32)


def tn_dot(a, b):
    return lax.dot_general(a, b, (((0,), (0,)), ((), ())), preferred_element_type=jnp.float32)


def attend_kernel(scalars, q_ref, k_ref, v_ref, out_ref):
    local_len = k_ref.shape[1]
    offset = scalars[0]
    start = scalars[1]
    rows = q_ref[...].astype(jnp.float32)
    pre_rows = rows[DEC:]
    pre_query = jnp.concatenate(
        [pre_rows[:, g * HD : (g + 1) * HD] for g in range(GROUP)], 0
    ).astype(jnp.bfloat16)

    def prefill(masked):
        token = lax.broadcasted_iota(jnp.int32, (1, LANES), 1) % PRE
        limit = start + token - offset
        top = jnp.full((1, LANES), FLOOR, jnp.float32)
        total = jnp.zeros((1, LANES), jnp.float32)
        acc = jnp.zeros((HD, LANES), jnp.float32)
        for tile in range(local_len // TILE):
            span = slice(tile * TILE, (tile + 1) * TILE)
            scores = nt_dot(k_ref[DEC, span], pre_query) * SCALE
            if masked:
                place = lax.broadcasted_iota(jnp.int32, (TILE, LANES), 0) + tile * TILE
                scores = jnp.where(place <= limit, scores, DEAD)
            new_top = jnp.maximum(top, jnp.max(scores, axis=0, keepdims=True))
            weights = jnp.exp2(scores - new_top)
            factor = jnp.exp2(top - new_top)
            total = total * factor + jnp.sum(weights, axis=0, keepdims=True)
            acc = acc * factor + tn_dot(v_ref[DEC, span], weights.astype(jnp.bfloat16))
            top = new_top
        stats = [*three_parts(top), *three_parts(total)]
        stats.append(jnp.zeros((2, LANES), jnp.float32))
        stats = jnp.concatenate(stats, 0)
        for j in range(2):
            lanes = slice(j * LANES // 2, (j + 1) * LANES // 2)
            out_ref[j, :HD, :] = acc[:, lanes].astype(jnp.bfloat16)
        return stats

    def decode():
        place = lax.broadcasted_iota(jnp.int32, (GROUP, local_len), 1)
        lane = lax.broadcasted_iota(jnp.int32, (GROUP, HD), 1)
        weighted, packed = [], []
        for b in range(DEC):
            query = jnp.concatenate(
                [rows[b : b + 1, g * HD : (g + 1) * HD] for g in range(GROUP)], 0
            ).astype(jnp.bfloat16)
            scores = nt_dot(query, k_ref[b]) * SCALE
            scores = jnp.where(place < scalars[2 + b] - offset, scores, DEAD)
            top = jnp.maximum(jnp.max(scores, axis=1, keepdims=True), FLOOR)
            weights = jnp.exp2(scores - top)
            total = jnp.sum(weights, axis=1, keepdims=True)
            weighted.append(
                jnp.dot(weights.astype(jnp.bfloat16), v_ref[b], preferred_element_type=jnp.float32)
            )
            stats = jnp.zeros((GROUP, HD), jnp.float32)
            for place_of, part in enumerate([*three_parts(top), *three_parts(total)]):
                stats = jnp.where(lane == place_of, part, stats)
            packed.append(stats)
        return jnp.concatenate(weighted, 1), jnp.concatenate(packed, 1)

    def finish(pre_stats):
        dec_weighted, dec_stats = decode()
        for j in range(2):
            heads = slice(j * HALF, (j + 1) * HALF)
            lanes = slice(j * LANES // 2, (j + 1) * LANES // 2)
            tail = jnp.concatenate(
                [
                    dec_weighted[heads],
                    pre_stats[:, lanes],
                    dec_stats[heads],
                    jnp.zeros((8, LANES // 2), jnp.float32),
                ],
                0,
            )
            out_ref[j, HD:, :] = tail.astype(jnp.bfloat16)

    whole = offset + local_len - 1 <= start

    @pl.when(whole)
    def _():
        finish(prefill(False))

    @pl.when(jnp.logical_not(whole))
    def _():
        finish(prefill(True))


def attend(scalars, queries, cache_k, cache_v):
    rows = queries.shape[0]
    sequences, local_len, _ = cache_k.shape
    return pl.pallas_call(
        attend_kernel,
        grid_spec=pltpu.PrefetchScalarGridSpec(
            num_scalar_prefetch=1,
            grid=(KVH,),
            in_specs=[
                pl.BlockSpec((rows, GROUP * HD), lambda h, s: (0, h)),
                pl.BlockSpec((sequences, local_len, HD), lambda h, s: (0, 0, h)),
                pl.BlockSpec((sequences, local_len, HD), lambda h, s: (0, 0, h)),
            ],
            out_specs=pl.BlockSpec((2, ROWS, LANES // 2), lambda h, s: (h, 0, 0)),
        ),
        out_shape=jax.ShapeDtypeStruct((2 * KVH, ROWS, LANES // 2), jnp.bfloat16),
        compiler_params=pltpu.CompilerParams(vmem_limit_bytes=48 * 1024 * 1024),
        name="attend",
    )(scalars, queries, cache_k, cache_v)


def join_kernel(parts_ref, out_ref):
    sources = parts_ref.shape[0]

    def stats_of(j, row):
        return parts_ref[j, HD:, :].astype(jnp.float32)[row : row + 8]

    pre_tops, pre_totals, dec_tops, dec_totals = [], [], [], []
    for j in range(sources):
        pre = stats_of(j, 8)
        pre_tops.append(pre[0:1] + pre[1:2] + pre[2:3])
        pre_totals.append(pre[3:4] + pre[4:5] + pre[5:6])
        dec = stats_of(j, 16)
        for tops, at in ((dec_tops, 0), (dec_totals, 3)):
            tops.append(
                [
                    sum(dec[:, b * HD + at + n : b * HD + at + n + 1] for n in range(3))
                    for b in range(DEC)
                ]
            )
    top = pre_tops[0]
    for other in pre_tops[1:]:
        top = jnp.maximum(top, other)
    total = jnp.zeros_like(top)
    acc = jnp.zeros((HD, LANES // 2), jnp.float32)
    for j in range(sources):
        factor = jnp.exp2(pre_tops[j] - top)
        total += factor * pre_totals[j]
        acc += factor * parts_ref[j, :HD, :].astype(jnp.float32)
    joined = (acc / total).T
    pre_out = jnp.concatenate([joined[g * PRE : (g + 1) * PRE] for g in range(HALF)], 1)
    dec_out = []
    for b in range(DEC):
        top = dec_tops[0][b]
        for other in dec_tops[1:]:
            top = jnp.maximum(top, other[b])
        total = jnp.zeros_like(top)
        acc = jnp.zeros((HALF, HD), jnp.float32)
        for j in range(sources):
            factor = jnp.exp2(dec_tops[j][b] - top)
            total += factor * dec_totals[j][b]
            acc += factor * stats_of(j, 0)[:, b * HD : (b + 1) * HD]
        joined = acc / total
        dec_out.append(jnp.concatenate([joined[g : g + 1] for g in range(HALF)], 1))
    out_ref[...] = jnp.concatenate([*dec_out, pre_out], 0).astype(jnp.bfloat16)


def join(parts):
    return pl.pallas_call(
        join_kernel,
        out_shape=jax.ShapeDtypeStruct((DEC + PRE, HALF * HD), jnp.bfloat16),
        in_specs=[pl.BlockSpec(memory_space=pltpu.VMEM)],
        out_specs=pl.BlockSpec(memory_space=pltpu.VMEM),
        compiler_params=pltpu.CompilerParams(vmem_limit_bytes=32 * 1024 * 1024),
        name="join",
    )(parts)


def on_device(queries, cache_k, cache_v, dec_lengths, pre_starts):
    local_len = cache_k.shape[2]
    offset = lax.axis_index("tensor") * local_len
    scalars = jnp.concatenate([offset[None], pre_starts, dec_lengths[0]]).astype(jnp.int32)
    parts = attend(scalars, queries[0], cache_k[0], cache_v[0])
    parts = lax.all_to_all(parts, "tensor", 0, 0, tiled=True)
    own_share = join(parts)
    count = lax.axis_size("pipe")
    pairs = [(source, (source + 1) % count) for source in range(count)]
    handed = lax.ppermute(own_share, "pipe", pairs)
    return handed[None]


def solution(mesh):
    in_specs = (
        P(("dp", "pipe"), None, None),
        P(("dp", "pipe"), None, "tensor", None),
        P(("dp", "pipe"), None, "tensor", None),
        P(("dp", "pipe"), None),
        P(("dp", "pipe")),
    )
    out_specs = P(("dp", "pipe"), None, "tensor")
    return jax.shard_map(
        on_device, mesh=mesh, in_specs=in_specs, out_specs=out_specs, check_vma=False
    )
```

time: 383 us -> 60.6 us (0.16)
  waiting for transfers between devices: 154 us -> 0.92 us
  local copies, waits for them, and re-layouts: 67.5 us -> 1.95 us
  other arithmetic: 61.2 us -> 0.73 us
  matrix products: 38.3 us -> 0 us
  Pallas kernels: 0 us -> 26.7 us
  blocking collectives: 44.4 us -> 27.9 us
  between operations: 14.2 us -> 0.67 us
    all_gather x1 -> x0, waiting for transfers between devices: 153 us -> none  [joined(): gathered = jax.tree.map(lambda a: lax.all_gather(a, axis), part)]
    all_gather x2 -> x0, blocking collectives: 44.4 us -> none  [joined(): gathered = jax.tree.map(lambda a: lax.all_gather(a, axis), part)]
    add x32 -> x0, other arithmetic: 43.1 us -> none  [the longest x15 42.7 us: combine(): first[0] * factor_first[..., None] + second[0] * factor_second[..., None]]
    dot_general x4 -> x0, matrix products: 38.3 us -> none  [the longest x1 16.4 us: on_device(): jnp.einsum('qkgd,pkd->qkgp', pre_query, pre_keys, preferred_element_type=...]
    unnamed x17 -> x3, local copies, waits for them, and re-layouts: 39.9 us -> 1.95 us
    all_to_all x0 -> x1, blocking collectives: none -> 27.9 us  [on_device(): parts = lax.all_to_all(parts, 'tensor', 0, 0, tiled=True)]
    pallas_call x0 -> x2, Pallas kernels: none -> 26.7 us  [the longest x1 26.3 us: attend(): pl.pallas_call(attend_kernel, grid_spec=pltpu.PrefetchScalarGridSpec(num_...]
    slice x4 -> x0, local copies, waits for them, and re-layouts: 24.3 us -> none  [the longest x1 7.58 us: on_device(): dec_values = value_cache[:dec_rows].reshape(dec_rows, local_len, KVH, HD)]
  transfers between devices with their start and end apart: 2 -> 1, of which waited for: 2 -> 1; matrix products, arithmetic and copies ran while one was open for 4% -> 0% of each run, Pallas kernels for 0% -> 0%
where the time goes in v1:
time: 60.6 us; the launch traced here: 60.4 us
  blocking collectives  27.9 us (46%)
  Pallas kernels  26.7 us (44%)
  local copies, waits for them, and re-layouts  1.95 us (3%)
  starting transfers between devices  1.45 us (2%)
  waiting for transfers between devices  0.92 us (2%)
  other arithmetic  0.73 us (1%)
  between operations  0.67 us (1%)
    all_to_all x1, blocking collectives, on_device(): parts = lax.all_to_all(parts, 'tensor', 0, 0, tiled=True)  27.9 us
    pallas_call x1, Pallas kernels, attend(): pl.pallas_call(attend_kernel, grid_spec=pltpu.PrefetchScalarGridSpec(num_...  26.3 us
    unnamed x3, local copies, waits for them, and re-layouts  1.95 us
    ppermute x1, starting transfers between devices, on_device(): handed = lax.ppermute(own_share, 'pipe', pairs)  1.45 us
  transfers between devices with their start and end apart: 1, of which 1 were waited for; matrix products, arithmetic and copies ran while one was open for 0% of the time, Pallas kernels for 0%

profile of v1, /device:TPU:1, one launch (start us, length us, event | category | flops | bytes accessed | tf_op | source)
XLA Modules:
  0.0 60.4 jit_solution(6374589933600492184)
XLA Ops:
  0.7 0.7 %pad_add_fusion.scalars = s32[4]{0:T(128)S(1)} fusion(s32[2]{0:T(128)} %bitcast.10, s32[1]{0:T(128)S(6)} %copy.7, s32[1]{0:T(128)} %bitcast), kind=kLoop, calls=%fused_computation | loop fusion | flops 8 | bytes 32 | tf_op jit(solution)/shard_map/concatenate | solution.py:206
  1.4 0.0 copy-start
  1.4 1.3 %copy-done = bf16[1,34,16384]{2,1,0:T(8,128)(2,1)S(1)} copy-done((bf16[1,34,16384]{2,1,0:T(8,128)(2,1)S(1)}, bf16[1,34,16384]{2,1,0:T(8,128)(2,1)}, u32[]{:S(2)}) %copy-start) | copy-done | bytes 1114136
  2.7 26.3 %attend.1 = bf16[16,160,256]{2,1,0:T(8,128)(2,1)S(1)} custom-call(s32[4]{0:T(128)S(1)} %pad_add_fusion.scalars, bf16[34,16384]{1,0:T(8,128)(2,1)S(1)} %bitcast.6, bf16[3,2048,1024]{2,1,0:T(8,128)(2,1)} %bitcast.7, bf16[3,2048,1024]{2,1,0:T(8,128)(2,1)} %bitcast.8), custom_call_target="tpu_custom_call" | custom-call | tf_op jit(solution)/shard_map/attend/pallas_call | solution.py:128
  29.0 27.9 %all_to_all.5.parts_ref = bf16[16,160,256]{2,1,0:T(8,128)(2,1)S(1)} all-to-all(bf16[16,160,256]{2,1,0:T(8,128)(2,1)S(1)} %attend.1), channel_id=1, replica_groups=mesh['dp'=4,'pipe'=2,'tensor'=16] {'tensor'}, dimensions={0} | all-to-all | bytes 2621440 | tf_op jit(solution)/shard_map/all_to_all | solution.py:208
  56.9 0.5 join.1
  57.4 1.5 %collective-permute-start = (bf16[34,1024]{1,0:T(8,128)(2,1)S(1)}, bf16[34,1024]{1,0:T(8,128)(2,1)S(1)}, u32[]{:S(2)}, u32[]{:S(2)}) collective-permute-start(bf16[34,1024]{1,0:T(8,128)(2,1)S(1)} %join.1), channel_id=1, source_target_pairs={{0,16},{16,0},{1,17},{17,1},{2,18},{18,2},{3,19},{19,3},{4,20},{20... | collective-permute-start | bytes 208904 | tf_op jit(solution)/shard_map/ppermute | solution.py:212
  58.8 0.9 %collective-permute-done = bf16[34,1024]{1,0:T(8,128)(2,1)S(1)} collective-permute-done((bf16[34,1024]{1,0:T(8,128)(2,1)S(1)}, bf16[34,1024]{1,0:T(8,128)(2,1)S(1)}, u32[]{:S(2)}, u32[]{:S(2)}) %collective-permute-start) | collective-permute-done | bytes 69664 | tf_op jit(solution)/shard_map/ppermute | solution.py:212
  59.8 0.6 %copy.8 = bf16[1,34,1024]{2,1,0:T(8,128)(2,1)} copy(bf16[1,34,1024]{2,1,0:T(8,128)(2,1)S(1)} %bitcast.9) | data formatting | bytes 139264
Async XLA Ops:
  1.4 1.3 %copy-start = (bf16[1,34,16384]{2,1,0:T(8,128)(2,1)S(1)}, bf16[1,34,16384]{2,1,0:T(8,128)(2,1)}, u32[]{:S(2)}) copy-start(bf16[1,34,16384]{2,1,0:T(8,128)(2,1)} %param.5) | copy-start | bytes 3342340
  57.4 2.4 %collective-permute-start = (bf16[34,1024]{1,0:T(8,128)(2,1)S(1)}, bf16[34,1024]{1,0:T(8,128)(2,1)S(1)}, u32[]{:S(2)}, u32[]{:S(2)}) collective-permute-start(bf16[34,1024]{1,0:T(8,128)(2,1)S(1)} %join.1), channel_id=1, source_target_pairs={{0,16},{16,0},{1,17},{17,1},{2,18},{18,2},{3,19},{19,3},{4,20},{20... | collective-permute-start | bytes 208904 | tf_op jit(solution)/shard_map/ppermute | solution.py:212

commit v2 on v0

v2 whole, which is shorter than its diff:
```python
import functools
import math

import jax
import jax.numpy as jnp
from jax import lax
from jax.experimental import pallas as pl
from jax.experimental.pallas import tpu as pltpu
from jax.sharding import PartitionSpec as P

HQ = 128
KVH = 8
HD = 128
GROUP = HQ // KVH
ACROSS = 4
HALF = GROUP // 2
DEC = 2
PRE = 32
LANES = GROUP * PRE
PAIR = 2
QK_TILE = 512
PV_TILE = 1024
ROWS = 160
SCALE = math.log2(math.e) / math.sqrt(HD)
DEAD = -1e30
FLOOR = -1e29
VMEM_LIMIT = 36 * 1024 * 1024
FETCHED = ("q", "k", "n", "v", "k0", "v0", "k1", "v1")
FIRST_SCHEDULE = "A0A1AA" "xBa0Ba0B0B" "Wb01b01" "111"
SCHEDULE = "A0A1AA" "Ba0Ba0B0B" "b01b01" "111"


def three_parts(x):
    first = x.astype(jnp.bfloat16).astype(jnp.float32)
    rest = x - first
    second = rest.astype(jnp.bfloat16).astype(jnp.float32)
    return first, second, rest - second


def nt_dot(a, b):
    return lax.dot_general(a, b, (((1,), (1,)), ((), ())), preferred_element_type=jnp.float32)


def tn_dot(a, b):
    return lax.dot_general(a, b, (((0,), (0,)), ((), ())), preferred_element_type=jnp.float32)


def scores_of(keys, query, s_ref, limit):
    local_len = keys.shape[0]
    top = jnp.full((1, LANES), FLOOR, jnp.float32)
    for at in range(0, local_len, QK_TILE):
        block = keys[at : at + QK_TILE]
        scores = nt_dot(jnp.concatenate([block, block], 1), query)
        if limit is not None:
            place = lax.broadcasted_iota(jnp.int32, (QK_TILE, LANES), 0) + at
            scores = jnp.where(place <= limit, scores, DEAD)
        s_ref[at : at + QK_TILE] = scores
        top = jnp.maximum(top, jnp.max(scores, axis=0, keepdims=True))
        yield top


def weighted_of(values, s_ref, top_of):
    local_len = values.shape[0]
    top = top_of()
    acc = None
    for at in range(0, local_len, PV_TILE):
        weights = jnp.exp2(s_ref[at : at + PV_TILE] - top).astype(jnp.bfloat16)
        block = jnp.concatenate(
            [values[at : at + PV_TILE].T, jnp.ones((16, PV_TILE), jnp.bfloat16)], 0
        )
        part = jnp.dot(block, weights, preferred_element_type=jnp.float32)
        acc = part if acc is None else acc + part
        yield acc


def decode_of(b, rows, k_ref, v_ref, length):
    local_len = k_ref.shape[1]
    blank = jnp.zeros((GROUP, HD), jnp.float32)
    query = []
    for n in range(PAIR):
        part = jnp.concatenate(
            [rows[b : b + 1, (n * GROUP + g) * HD : (n * GROUP + g + 1) * HD] for g in range(GROUP)], 0
        )
        query.append(jnp.concatenate([part if n == m else blank for m in range(PAIR)], 1))
    query = jnp.concatenate(query, 0).astype(jnp.bfloat16)
    yield
    scores = nt_dot(query, k_ref[b]) * SCALE
    yield
    place = lax.broadcasted_iota(jnp.int32, (GROUP * PAIR, local_len), 1)
    scores = jnp.where(place < length, scores, DEAD)
    top = jnp.maximum(jnp.max(scores, axis=1, keepdims=True), FLOOR)
    yield
    weights = jnp.exp2(scores - top)
    total = jnp.sum(weights, axis=1, keepdims=True)
    yield
    both = jnp.dot(weights.astype(jnp.bfloat16), v_ref[b], preferred_element_type=jnp.float32)
    yield
    weighted = jnp.concatenate(
        [both[n * GROUP : (n + 1) * GROUP, n * HD : (n + 1) * HD] for n in range(PAIR)], 0
    )
    yield weighted, top, total


def place_of_device():
    place = lax.axis_index("tensor")
    return lax.axis_index("pipe"), place // ACROSS, place % ACROSS


def moved(here, by):
    return lax.rem(here + by, ACROSS)


def fetches(shift, sources, targets, sems):
    section, slow, _ = place_of_device()
    pair = moved(slow, jnp.where(section == 0, shift[0], shift[1]))
    q_hbm, k_hbm, v_hbm = sources
    q_ref, k_ref, v_ref = targets

    def columns(count):
        return pl.ds(pl.multiple_of(pair * count, count), count)

    moves = {"q": (q_hbm.at[:, columns(PAIR * GROUP * HD)], q_ref)}
    for name, sequence in (("", DEC), *((str(b), b) for b in range(DEC))):
        for kind, hbm, ref in (("k", k_hbm, k_ref), ("v", v_hbm, v_ref)):
            moves[kind + name] = (hbm.at[sequence, :, columns(PAIR * HD)], ref.at[sequence])
    return {
        name: pltpu.make_async_copy(*move, sems.at[n]) for n, (name, move) in enumerate(moves.items())
    }


def attend_kernel(shift, after, *refs):
    refs = list(refs)

    def take(count):
        return [refs.pop(0) for _ in range(count)]

    first = shift == ORDER[0]
    (starts,) = take(1)
    if first:
        (lengths_hbm,) = take(1)
    else:
        (lengths_ref,) = take(1)
        held = take(3)
    sources = take(3) if first or after is not None else None
    (out_ref,) = take(1)
    if first:
        (lengths_ref,) = take(1)
    coming = take(3) if after is not None else None
    s_first, s_second, sems, later_sems = take(4)
    if first:
        lengths, *held = take(4)
    q_ref, k_ref, v_ref = held
    local_len = k_ref.shape[1]
    offset = lax.axis_index("tensor") * local_len

    waiting = {}
    if first:
        waiting = fetches(shift, sources, held, sems)
        waiting["n"] = pltpu.make_async_copy(lengths_hbm, lengths, sems.at[len(waiting)])
        for name in FETCHED:
            waiting[name].start()
    later = fetches(after, sources, coming, later_sems) if after is not None else {}

    def start_later():
        for copy in later.values():
            copy.start()

    if not first:
        start_later()

    @pl.when(starts[0] >= 0)
    def _():
        def wait(names):
            for name in names:
                if name in waiting:
                    waiting.pop(name).wait()

        wait(("q",))
        rows = q_ref[...].astype(jnp.float32)
        pre_rows = rows[DEC:] * SCALE
        queries = []
        for n in range(PAIR):
            query = jnp.concatenate(
                [pre_rows[:, (n * GROUP + g) * HD : (n * GROUP + g + 1) * HD] for g in range(GROUP)], 0
            )
            high = query.astype(jnp.bfloat16)
            low = (query - high.astype(jnp.float32)).astype(jnp.bfloat16)
            queries.append(jnp.concatenate([high, low], 1))
        wait(("n", "k"))
        if first:
            start_later()
        token = lax.broadcasted_iota(jnp.int32, (1, LANES), 1) % PRE
        limit = starts[0] + token - offset
        if first:
            row = lax.broadcasted_iota(jnp.int32, lengths_ref.shape, 0)
            lengths_ref[...] = functools.reduce(
                lambda rest, b: jnp.where(row == b, lengths[0, b], rest), range(DEC), jnp.zeros_like(row)
            )

        def keys(n):
            return k_ref.at[DEC, :, n * HD : (n + 1) * HD]

        def values(n):
            return v_ref.at[DEC, :, n * HD : (n + 1) * HD]

        last = {}
        streams = {
            "A": scores_of(keys(0), queries[0], s_first, limit),
            "B": scores_of(keys(1), queries[1], s_second, limit),
            "a": weighted_of(values(0), s_first, lambda: last["A"]),
            "b": weighted_of(values(1), s_second, lambda: last["B"]),
        }
        for b in range(DEC):
            length = lengths[0, b] if first else lengths_ref[b : b + 1, 0:1]
            streams[str(b)] = decode_of(b, rows, k_ref, v_ref, length - offset)
        for name in FIRST_SCHEDULE if first else SCHEDULE:
            if name == "x":
                wait(("v", "k0"))
            elif name == "W":
                wait(list(waiting))
            else:
                last[name] = next(streams[name])
        dec_first, dec_second = last["0"], last["1"]
        top_first, acc_first, top_second, acc_second = (last[name] for name in "AaBb")
        for n, (top, acc) in enumerate(((top_first, acc_first), (top_second, acc_second))):
            for j in range(2):
                heads = slice(n * GROUP + j * HALF, n * GROUP + (j + 1) * HALF)
                lanes = slice(j * LANES // 2, (j + 1) * LANES // 2)
                out_ref[2 * n + j] = packed(
                    acc[:HD, lanes],
                    top[:, lanes],
                    acc[HD : HD + 1, lanes],
                    [[part[heads] for part in one] for one in (dec_first, dec_second)],
                )
    for copy in later.values():
        copy.wait()


def packed(acc, top, total, dec):
    lane = lax.broadcasted_iota(jnp.int32, (HALF, HD), 1)
    dec_stats = []
    for _, dec_top, dec_total in dec:
        stats = jnp.zeros((HALF, HD), jnp.float32)
        for place_of, part in enumerate([*three_parts(dec_top), *three_parts(dec_total)]):
            stats = jnp.where(lane == place_of, part, stats)
        dec_stats.append(stats)
    return jnp.concatenate(
        [
            acc,
            jnp.concatenate([one[0] for one in dec], 1),
            *three_parts(top),
            *three_parts(total),
            jnp.zeros((2, LANES // 2), jnp.float32),
            jnp.concatenate(dec_stats, 1),
            jnp.zeros((8, LANES // 2), jnp.float32),
        ],
        0,
    ).astype(jnp.bfloat16)


def attend(shift, after, starts, lengths, held, sources):
    first = shift == ORDER[0]
    queries, cache_k, _ = sources
    rows = queries.shape[0]
    sequences, local_len, _ = cache_k.shape
    operands = [
        ((rows, PAIR * GROUP * HD), queries.dtype),
        ((sequences, local_len, PAIR * HD), cache_k.dtype),
        ((sequences, local_len, PAIR * HD), cache_k.dtype),
    ]
    args = [starts, lengths, *held]
    in_specs = [pl.BlockSpec(memory_space=pltpu.SMEM)]
    in_specs += [pl.BlockSpec(memory_space=pl.ANY if first else pltpu.VMEM)] * (1 + len(held))
    if first or after is not None:
        args += sources
        in_specs += [pl.BlockSpec(memory_space=pl.ANY)] * 3
    outs = [pltpu.VMEM((ACROSS, ROWS, LANES // 2), jnp.bfloat16)]
    if first:
        outs.append(pltpu.VMEM((8, HD), jnp.int32))
    if after is not None:
        outs += [pltpu.VMEM(*operand) for operand in operands]
    scratch = [
        pltpu.VMEM((local_len, LANES), jnp.float32),
        pltpu.VMEM((local_len, LANES), jnp.float32),
        pltpu.SemaphoreType.DMA((2 * sequences + 2,)),
        pltpu.SemaphoreType.DMA((2 * sequences + 2,)),
    ]
    if first:
        scratch.append(pltpu.SMEM(lengths.shape, jnp.int32))
        scratch += [pltpu.VMEM(*operand) for operand in operands]
    part, *rest = pl.pallas_call(
        functools.partial(attend_kernel, shift, after),
        in_specs=in_specs,
        out_specs=[pl.BlockSpec(memory_space=pltpu.VMEM)] * len(outs),
        out_shape=outs,
        scratch_shapes=scratch,
        compiler_params=pltpu.CompilerParams(vmem_limit_bytes=VMEM_LIMIT),
        cost_estimate=pl.CostEstimate(
            flops=4 * PAIR * GROUP * HD * (PRE + DEC) * local_len,
            bytes_accessed=4 * sequences * local_len * PAIR * HD,
            transcendentals=PAIR * GROUP * (PRE + DEC) * local_len,
        ),
        name="attend",
    )(*args)
    if first:
        lengths, *rest = rest
    return part, lengths, rest


def joined(parts):
    def add(tops, totals, sums):
        top = functools.reduce(jnp.maximum, tops)
        factors = [jnp.exp2(one - top) for one in tops]
        total = sum(factor * one for factor, one in zip(factors, totals))
        return sum(factor * one for factor, one in zip(factors, sums)), top, total

    tails = [part[HD:, :].astype(jnp.float32) for part in parts]
    stats = [tail[8:16] for tail in tails]
    pre = add(
        [one[0:1] + one[1:2] + one[2:3] for one in stats],
        [one[3:4] + one[4:5] + one[5:6] for one in stats],
        [part[:HD, :].astype(jnp.float32) for part in parts],
    )
    dec = []
    for b in range(DEC):
        at = b * HD
        stats = [tail[16:24] for tail in tails]
        dec.append(
            add(
                [sum(one[:, at + n : at + n + 1] for n in range(3)) for one in stats],
                [sum(one[:, at + n : at + n + 1] for n in range(3, 6)) for one in stats],
                [tail[:8, at : at + HD] for tail in tails],
            )
        )
    return pre, dec


def join_some_kernel(*refs):
    parts, outs = refs[:ACROSS], refs[ACROSS:]
    _, _, fast = place_of_device()
    for by, out in zip(FAST_ORDER, outs):
        target = moved(fast, by)
        pre, dec = joined([part.at[target] for part in parts])
        out[...] = packed(*pre, dec)


def join_some(parts):
    return pl.pallas_call(
        join_some_kernel,
        in_specs=[pl.BlockSpec(memory_space=pltpu.VMEM)] * ACROSS,
        out_specs=[pl.BlockSpec(memory_space=pltpu.VMEM)] * ACROSS,
        out_shape=[jax.ShapeDtypeStruct((ROWS, LANES // 2), jnp.bfloat16)] * ACROSS,
        compiler_params=pltpu.CompilerParams(vmem_limit_bytes=32 * 1024 * 1024),
        name="join_some",
    )(*parts)


def join_last_kernel(*refs):
    (acc, _, total), dec = joined(refs[:-1])
    result = (acc / total).T
    rows = []
    for dec_acc, _, dec_total in dec:
        one = dec_acc / dec_total
        rows.append(jnp.concatenate([one[g : g + 1] for g in range(HALF)], 1))
    rows.append(jnp.concatenate([result[g * PRE : (g + 1) * PRE] for g in range(HALF)], 1))
    refs[-1][...] = jnp.concatenate(rows, 0).astype(jnp.bfloat16)


def join_last(parts):
    return pl.pallas_call(
        join_last_kernel,
        in_specs=[pl.BlockSpec(memory_space=pltpu.VMEM)] * ACROSS,
        out_specs=pl.BlockSpec(memory_space=pltpu.VMEM),
        out_shape=jax.ShapeDtypeStruct((DEC + PRE, HALF * HD), jnp.bfloat16),
        compiler_params=pltpu.CompilerParams(vmem_limit_bytes=32 * 1024 * 1024),
        name="join_last",
    )(*parts)


def sent(value, step):
    sections = lax.axis_size("pipe")
    pairs = []
    for section in range(sections):
        by_section, by_slow, by_fast = step(section)
        to_section = (section + by_section) % sections
        for slow in range(ACROSS):
            for fast in range(ACROSS):
                to = ((slow + by_slow) % ACROSS) * ACROSS + (fast + by_fast) % ACROSS
                here = (section * ACROSS + slow) * ACROSS + fast
                pairs.append((here, to_section * ACROSS * ACROSS + to))
    return lax.ppermute(value, ("pipe", "tensor"), pairs)


ORDER = ((2, 2), (3, 1), (1, 3), (0, 0))
FAST_ORDER = (2, 1, 3, 0)


def on_device(queries, cache_k, cache_v, dec_lengths, pre_starts):
    sources = [
        pltpu.with_memory_space_constraint(one, pltpu.HBM) for one in (queries[0], cache_k[0], cache_v[0])
    ]
    lengths = pltpu.with_memory_space_constraint(dec_lengths, pltpu.HBM)
    held, parts = [], []
    for shift, after in zip(ORDER, (*ORDER[1:], None)):
        part, lengths, held = attend(shift, after, pre_starts, lengths, held, sources)
        if shift != (0, 0):
            part = sent(part, lambda section, shift=shift: (0, shift[section % 2], 0))
        parts.append(part)
    shares = join_some(parts)
    shares = [sent(share, lambda section, by=by: (1, 0, by)) for by, share in zip(FAST_ORDER, shares)]
    return join_last(shares)[None]


def solution(mesh):
    in_specs = (
        P(("dp", "pipe"), None, None),
        P(("dp", "pipe"), None, "tensor", None),
        P(("dp", "pipe"), None, "tensor", None),
        P(("dp", "pipe"), None),
        P(("dp", "pipe")),
    )
    out_specs = P(("dp", "pipe"), None, "tensor")
    return jax.shard_map(
        on_device, mesh=mesh, in_specs=in_specs, out_specs=out_specs, check_vma=False
    )
```

time: 383 us -> 38.8 us (0.10)
  waiting for transfers between devices: 154 us -> 2.63 us
  local copies, waits for them, and re-layouts: 67.5 us -> 0 us
  other arithmetic: 61.2 us -> 0 us
  blocking collectives: 44.4 us -> 0 us
  matrix products: 38.3 us -> 0 us
  Pallas kernels: 0 us -> 19.4 us
  starting transfers between devices: 0.76 us -> 15.9 us
  between operations: 14.2 us -> 0.71 us
    all_gather x1 -> x0, waiting for transfers between devices: 153 us -> none  [joined(): gathered = jax.tree.map(lambda a: lax.all_gather(a, axis), part)]
    all_gather x2 -> x0, blocking collectives: 44.4 us -> none  [joined(): gathered = jax.tree.map(lambda a: lax.all_gather(a, axis), part)]
    add x32 -> x0, other arithmetic: 43.1 us -> none  [the longest x15 42.7 us: combine(): first[0] * factor_first[..., None] + second[0] * factor_second[..., None]]
    unnamed x17 -> x0, local copies, waits for them, and re-layouts: 39.9 us -> none
    dot_general x4 -> x0, matrix products: 38.3 us -> none  [the longest x1 16.4 us: on_device(): jnp.einsum('qkgd,pkd->qkgp', pre_query, pre_keys, preferred_element_type=...]
    slice x4 -> x0, local copies, waits for them, and re-layouts: 24.3 us -> none  [the longest x1 7.58 us: on_device(): dec_values = value_cache[:dec_rows].reshape(dec_rows, local_len, KVH, HD)]
    pallas_call x0 -> x6, Pallas kernels: none -> 19.4 us  [the longest x4 18 us: attend(): pl.pallas_call(functools.partial(attend_kernel, shift, after), in_specs=i...]
    reduce_sum x2 -> x0, other arithmetic: 16.2 us -> none  [partial_softmax(): return (weights.astype(jnp.bfloat16), maxima, jnp.sum(weights, axis=-1))]
  transfers between devices with their start and end apart: 2 -> 7, of which waited for: 2 -> 2; matrix products, arithmetic and copies ran while one was open for 4% -> 0% of each run, Pallas kernels for 0% -> 32%
where the time goes in v2:
time: 38.8 us; the launch traced here: 38.7 us
  Pallas kernels  19.4 us (50%)
  starting transfers between devices  15.9 us (41%)
  waiting for transfers between devices  2.63 us (7%)
  between operations  0.71 us (2%)
    pallas_call x4, Pallas kernels, attend(): pl.pallas_call(functools.partial(attend_kernel, shift, after), in_specs=i...  18 us
    ppermute x7, starting transfers between devices, sent(): return lax.ppermute(value, ('pipe', 'tensor'), pairs)  15.9 us
    ppermute x7, waiting for transfers between devices, sent(): return lax.ppermute(value, ('pipe', 'tensor'), pairs)  2.63 us
    pallas_call x1, Pallas kernels, join_last(): pl.pallas_call(join_last_kernel, in_specs=[pl.BlockSpec(memory_space=pltp...  0.87 us
  transfers between devices with their start and end apart: 7, of which 2 were waited for; matrix products, arithmetic and copies ran while one was open for 0% of the time, Pallas kernels for 32%

profile of v2, /device:TPU:1, one launch (start us, length us, event | category | flops | bytes accessed | tf_op | source)
XLA Modules:
  0.0 38.7 jit_solution(12692048313541030977)
XLA Ops:
  0.7 5.5 %attend.4 = (bf16[4,160,256]{2,1,0:T(8,128)(2,1)S(1)}, s32[8,128]{1,0:T(8,128)S(1)}, bf16[34,4096]{1,0:T(8,128)(2,1)S(1)}, bf16[3,2048,256]{2,1,0:T(8,128)(2,1)S(1)}, bf16[3,2048,256]{2,1,0:T(8,128)(2,1)S(1)}) custom-call(s32[1]{0:T(128)S(6)} %copy.6.refs_0_, s32[1,2]{1,0:T(1,128)} %refs_1_.1, bf16[34,16384]{1,0:T(8,128)(2,1)} %bitcast.10, ...), custom_call_target="tpu_custom_call" | custom-call | flops 1140850688 | bytes 6291456 | tf_op jit(solution)/shard_map/attend/pallas_call | solution.py:291
  6.2 4.5 %collective-permute-start = (bf16[4,160,256]{2,1,0:T(8,128)(2,1)S(1)}, bf16[4,160,256]{2,1,0:T(8,128)(2,1)S(1)}, u32[]{:S(2)}, u32[]{:S(2)}) collective-permute-start(bf16[4,160,256]{2,1,0:T(8,128)(2,1)S(1)} %get-tuple-element.22), channel_id=1, source_target_pairs={{0,8},{1,9},{2,10},{3,11},{4,12},{5,13},{6,14},{7,15},{8,0},{9,1},... | collective-permute-start | bytes 983048 | tf_op jit(solution)/shard_map/ppermute | solution.py:391
  10.7 4.2 %attend.5 = (bf16[4,160,256]{2,1,0:T(8,128)(2,1)S(1)}, bf16[34,4096]{1,0:T(8,128)(2,1)S(1)}, bf16[3,2048,256]{2,1,0:T(8,128)(2,1)S(1)}, bf16[3,2048,256]{2,1,0:T(8,128)(2,1)S(1)}) custom-call(s32[1]{0:T(128)S(6)} %copy.6.refs_0_, s32[8,128]{1,0:T(8,128)S(1)} %get-tuple-element.23.refs_1_, bf16[34,4096]{1,0:T(8,128)(2,1)S(1)} %get-tuple-element.24.refs_2_, ...), custom_call_target="tpu_custom_call" | custom-call | flops 1140850688 | bytes 6291456 | tf_op jit(solution)/shard_map/attend/pallas_call | solution.py:291
  14.9 0.8 %collective-permute-start.1 = (bf16[4,160,256]{2,1,0:T(8,128)(2,1)S(1)}, bf16[4,160,256]{2,1,0:T(8,128)(2,1)S(1)}, u32[]{:S(2)}, u32[]{:S(2)}) collective-permute-start(bf16[4,160,256]{2,1,0:T(8,128)(2,1)S(1)} %get-tuple-element.27), channel_id=1, source_target_pairs={{0,12},{1,13},{2,14},{3,15},{4,0},{5,1},{6,2},{7,3},{8,4},{9,5},{1... | collective-permute-start | bytes 983048 | tf_op jit(solution)/shard_map/ppermute | solution.py:391
  15.7 4.2 %attend.6 = (bf16[4,160,256]{2,1,0:T(8,128)(2,1)S(1)}, bf16[34,4096]{1,0:T(8,128)(2,1)S(1)}, bf16[3,2048,256]{2,1,0:T(8,128)(2,1)S(1)}, bf16[3,2048,256]{2,1,0:T(8,128)(2,1)S(1)}) custom-call(s32[1]{0:T(128)S(6)} %copy.6.refs_0_, s32[8,128]{1,0:T(8,128)S(1)} %get-tuple-element.23.refs_1_, bf16[34,4096]{1,0:T(8,128)(2,1)S(1)} %get-tuple-element.28.refs_2_, ...), custom_call_target="tpu_custom_call" | custom-call | flops 1140850688 | bytes 6291456 | tf_op jit(solution)/shard_map/attend/pallas_call | solution.py:291
  19.9 2.2 %collective-permute-start.2 = (bf16[4,160,256]{2,1,0:T(8,128)(2,1)S(1)}, bf16[4,160,256]{2,1,0:T(8,128)(2,1)S(1)}, u32[]{:S(2)}, u32[]{:S(2)}) collective-permute-start(bf16[4,160,256]{2,1,0:T(8,128)(2,1)S(1)} %get-tuple-element.31), channel_id=1, source_target_pairs={{0,4},{1,5},{2,6},{3,7},{4,8},{5,9},{6,10},{7,11},{8,12},{9,13},{1... | collective-permute-start | bytes 983048 | tf_op jit(solution)/shard_map/ppermute | solution.py:391
  22.1 4.1 %attend.7.refs_3_ = bf16[4,160,256]{2,1,0:T(8,128)(2,1)S(1)} custom-call(s32[1]{0:T(128)S(6)} %copy.6.refs_0_, s32[8,128]{1,0:T(8,128)S(1)} %get-tuple-element.23.refs_1_, bf16[34,4096]{1,0:T(8,128)(2,1)S(1)} %get-tuple-element.32.refs_2_, bf16[3,2048,256]{2,1,0:T(8,128)(2,1)S(1)} %get-tuple-element.33.refs_3_, ...), custom_call_target="tpu_custom_call" | custom-call | flops 1140850688 | bytes 6291456 | tf_op jit(solution)/shard_map/attend/pallas_call | solution.py:291
  26.2 0.0 collective-permute-done.refs_0_
  26.2 0.0 collective-permute-done.1.refs_1_
  26.2 0.5 %collective-permute-done.2.refs_2_ = bf16[4,160,256]{2,1,0:T(8,128)(2,1)S(1)} collective-permute-done((bf16[4,160,256]{2,1,0:T(8,128)(2,1)S(1)}, bf16[4,160,256]{2,1,0:T(8,128)(2,1)S(1)}, u32[]{:S(2)}, u32[]{:S(2)}) %collective-permute-start.2) | collective-permute-done | bytes 327712 | tf_op jit(solution)/shard_map/ppermute | solution.py:391
  26.7 0.5 %join_some.1 = (bf16[160,256]{1,0:T(8,128)(2,1)S(1)}, bf16[160,256]{1,0:T(8,128)(2,1)S(1)}, bf16[160,256]{1,0:T(8,128)(2,1)S(1)}, bf16[160,256]{1,0:T(8,128)(2,1)S(1)}) custom-call(bf16[4,160,256]{2,1,0:T(8,128)(2,1)S(1)} %collective-permute-done.refs_0_, bf16[4,160,256]{2,1,0:T(8,128)(2,1)S(1)} %collective-permute-done.1.refs_1_, ...), custom_call_target="tpu_custom_call" | custom-call | tf_op jit(solution)/shard_map/join_some/pallas_call | solution.py:348
  27.2 5.5 %collective-permute-start.3 = (bf16[160,256]{1,0:T(8,128)(2,1)S(1)}, bf16[160,256]{1,0:T(8,128)(2,1)S(1)}, u32[]{:S(2)}, u32[]{:S(2)}) collective-permute-start(bf16[160,256]{1,0:T(8,128)(2,1)S(1)} %get-tuple-element.35), channel_id=1, source_target_pairs={{0,18},{1,19},{2,16},{3,17},{4,22},{5,23},{6,20},{7,21},{8,26},{9,... | collective-permute-start | bytes 245768 | tf_op jit(solution)/shard_map/ppermute | solution.py:391
  32.7 0.0 collective-permute-start.4
  32.7 3.0 %collective-permute-start.5 = (bf16[160,256]{1,0:T(8,128)(2,1)S(1)}, bf16[160,256]{1,0:T(8,128)(2,1)S(1)}, u32[]{:S(2)}, u32[]{:S(2)}) collective-permute-start(bf16[160,256]{1,0:T(8,128)(2,1)S(1)} %get-tuple-element.37), channel_id=1, source_target_pairs={{0,19},{1,16},{2,17},{3,18},{4,23},{5,20},{6,21},{7,22},{8,27},{9,... | collective-permute-start | bytes 245768 | tf_op jit(solution)/shard_map/ppermute | solution.py:391
  35.7 0.0 collective-permute-start.6
  35.7 0.0 collective-permute-done.3.refs_0_
  35.7 2.1 %collective-permute-done.4.refs_1_ = bf16[160,256]{1,0:T(8,128)(2,1)S(1)} collective-permute-done((bf16[160,256]{1,0:T(8,128)(2,1)S(1)}, bf16[160,256]{1,0:T(8,128)(2,1)S(1)}, u32[]{:S(2)}, u32[]{:S(2)}) %collective-permute-start.4) | collective-permute-done | bytes 81952 | tf_op jit(solution)/shard_map/ppermute | solution.py:391
  37.8 0.0 collective-permute-done.5.refs_2_
  37.8 0.0 collective-permute-done.6.refs_3_
  37.8 0.9 %join_last.1 = bf16[34,1024]{1,0:T(8,128)(2,1)} custom-call(bf16[160,256]{1,0:T(8,128)(2,1)S(1)} %collective-permute-done.3.refs_0_, bf16[160,256]{1,0:T(8,128)(2,1)S(1)} %collective-permute-done.4.refs_1_, bf16[160,256]{1,0:T(8,128)(2,1)S(1)} %collective-permute-done.5.refs_2_, bf16[160,256]{1,0:T(8,128)(2,1)S(1)} %collective-permute-done.6.refs_3_), custom_call_target="tpu_custom_call" | custom-call | tf_op jit(solution)/shard_map/join_last/pallas_call | solution.py:370
Async XLA Ops:
  6.2 20.0 %collective-permute-start = (bf16[4,160,256]{2,1,0:T(8,128)(2,1)S(1)}, bf16[4,160,256]{2,1,0:T(8,128)(2,1)S(1)}, u32[]{:S(2)}, u32[]{:S(2)}) collective-permute-start(bf16[4,160,256]{2,1,0:T(8,128)(2,1)S(1)} %get-tuple-element.22), channel_id=1, source_target_pairs={{0,8},{1,9},{2,10},{3,11},{4,12},{5,13},{6,14},{7,15},{8,0},{9,1},... | collective-permute-start | bytes 983048 | tf_op jit(solution)/shard_map/ppermute | solution.py:391
  14.9 11.3 %collective-permute-start.1 = (bf16[4,160,256]{2,1,0:T(8,128)(2,1)S(1)}, bf16[4,160,256]{2,1,0:T(8,128)(2,1)S(1)}, u32[]{:S(2)}, u32[]{:S(2)}) collective-permute-start(bf16[4,160,256]{2,1,0:T(8,128)(2,1)S(1)} %get-tuple-element.27), channel_id=1, source_target_pairs={{0,12},{1,13},{2,14},{3,15},{4,0},{5,1},{6,2},{7,3},{8,4},{9,5},{1... | collective-permute-start | bytes 983048 | tf_op jit(solution)/shard_map/ppermute | solution.py:391
  19.9 6.9 %collective-permute-start.2 = (bf16[4,160,256]{2,1,0:T(8,128)(2,1)S(1)}, bf16[4,160,256]{2,1,0:T(8,128)(2,1)S(1)}, u32[]{:S(2)}, u32[]{:S(2)}) collective-permute-start(bf16[4,160,256]{2,1,0:T(8,128)(2,1)S(1)} %get-tuple-element.31), channel_id=1, source_target_pairs={{0,4},{1,5},{2,6},{3,7},{4,8},{5,9},{6,10},{7,11},{8,12},{9,13},{1... | collective-permute-start | bytes 983048 | tf_op jit(solution)/shard_map/ppermute | solution.py:391
  27.2 8.5 %collective-permute-start.3 = (bf16[160,256]{1,0:T(8,128)(2,1)S(1)}, bf16[160,256]{1,0:T(8,128)(2,1)S(1)}, u32[]{:S(2)}, u32[]{:S(2)}) collective-permute-start(bf16[160,256]{1,0:T(8,128)(2,1)S(1)} %get-tuple-element.35), channel_id=1, source_target_pairs={{0,18},{1,19},{2,16},{3,17},{4,22},{5,23},{6,20},{7,21},{8,26},{9,... | collective-permute-start | bytes 245768 | tf_op jit(solution)/shard_map/ppermute | solution.py:391
  32.7 5.1 %collective-permute-start.4 = (bf16[160,256]{1,0:T(8,128)(2,1)S(1)}, bf16[160,256]{1,0:T(8,128)(2,1)S(1)}, u32[]{:S(2)}, u32[]{:S(2)}) collective-permute-start(bf16[160,256]{1,0:T(8,128)(2,1)S(1)} %get-tuple-element.36), channel_id=1, source_target_pairs={{0,17},{1,18},{2,19},{3,16},{4,21},{5,22},{6,23},{7,20},{8,25},{9,... | collective-permute-start | bytes 245768 | tf_op jit(solution)/shard_map/ppermute | solution.py:391
  32.7 5.1 %collective-permute-start.5 = (bf16[160,256]{1,0:T(8,128)(2,1)S(1)}, bf16[160,256]{1,0:T(8,128)(2,1)S(1)}, u32[]{:S(2)}, u32[]{:S(2)}) collective-permute-start(bf16[160,256]{1,0:T(8,128)(2,1)S(1)} %get-tuple-element.37), channel_id=1, source_target_pairs={{0,19},{1,16},{2,17},{3,18},{4,23},{5,20},{6,21},{7,22},{8,27},{9,... | collective-permute-start | bytes 245768 | tf_op jit(solution)/shard_map/ppermute | solution.py:391
  35.7 2.1 %collective-permute-start.6 = (bf16[160,256]{1,0:T(8,128)(2,1)S(1)}, bf16[160,256]{1,0:T(8,128)(2,1)S(1)}, u32[]{:S(2)}, u32[]{:S(2)}) collective-permute-start(bf16[160,256]{1,0:T(8,128)(2,1)S(1)} %get-tuple-element.38), channel_id=1, source_target_pairs={{0,16},{1,17},{2,18},{3,19},{4,20},{5,21},{6,22},{7,23},{8,24},{9,... | collective-permute-start | bytes 245768 | tf_op jit(solution)/shard_map/ppermute | solution.py:391

commit v3 on v2

--- a/solution.py
+++ b/solution.py
@@ -20,7 +20,7 @@
 PAIR = 2
 QK_TILE = 512
 PV_TILE = 1024
-ROWS = 160
+ROWS = 144
 SCALE = math.log2(math.e) / math.sqrt(HD)
 DEAD = -1e30
 FLOOR = -1e29
@@ -237,25 +237,27 @@
 
 
 def packed(acc, top, total, dec):
-    lane = lax.broadcasted_iota(jnp.int32, (HALF, HD), 1)
     dec_stats = []
     for _, dec_top, dec_total in dec:
-        stats = jnp.zeros((HALF, HD), jnp.float32)
-        for place_of, part in enumerate([*three_parts(dec_top), *three_parts(dec_total)]):
-            stats = jnp.where(lane == place_of, part, stats)
-        dec_stats.append(stats)
+        parts = [*three_parts(dec_top), *three_parts(dec_total)]
+        stats = sum(jnp.where(in_lanes(n), part, 0.0) for n, part in enumerate(parts))
+        dec_stats.append(jnp.sum(stats, axis=0, keepdims=True))
     return jnp.concatenate(
         [
             acc,
             jnp.concatenate([one[0] for one in dec], 1),
             *three_parts(top),
             *three_parts(total),
-            jnp.zeros((2, LANES // 2), jnp.float32),
             jnp.concatenate(dec_stats, 1),
-            jnp.zeros((8, LANES // 2), jnp.float32),
+            jnp.zeros((1, LANES // 2), jnp.float32),
         ],
         0,
     ).astype(jnp.bfloat16)
+
+
+def in_lanes(n):
+    row = lax.broadcasted_iota(jnp.int32, (HALF, HD), 0)
+    return lax.broadcasted_iota(jnp.int32, (HALF, HD), 1) == n * HALF + row
 
 
 def attend(shift, after, starts, lengths, held, sources):
@@ -323,13 +325,18 @@
     )
     dec = []
     for b in range(DEC):
-        at = b * HD
-        stats = [tail[16:24] for tail in tails]
+        lanes = slice(b * HD, (b + 1) * HD)
+        stats = [tail[14:15, lanes] for tail in tails]
+
+        def column(stat, places):
+            mask = functools.reduce(jnp.logical_or, [in_lanes(n) for n in places])
+            return jnp.sum(jnp.where(mask, stat, 0.0), axis=1, keepdims=True)
+
         dec.append(
             add(
-                [sum(one[:, at + n : at + n + 1] for n in range(3)) for one in stats],
-                [sum(one[:, at + n : at + n + 1] for n in range(3, 6)) for one in stats],
-                [tail[:8, at : at + HD] for tail in tails],
+                [column(stat, range(3)) for stat in stats],
+                [column(stat, range(3, 6)) for stat in stats],
+                [tail[:8, lanes] for tail in tails],
             )
         )
     return pre, dec
@@ -337,7 +344,7 @@
 
 def join_some_kernel(*refs):
     parts, outs = refs[:ACROSS], refs[ACROSS:]
-    _, _, fast = place_of_device()
+    section, _, fast = place_of_device()
     for by, out in zip(FAST_ORDER, outs):
         target = moved(fast, by)
         pre, dec = joined([part.at[target] for part in parts])

time: 38.8 us -> 38.2 us (0.985)
  waiting for transfers between devices: 2.63 us -> 2.04 us
    ppermute x7, waiting for transfers between devices: 2.63 us -> 2.04 us  [sent(): return lax.ppermute(value, ('pipe', 'tensor'), pairs)]
  transfers between devices with their start and end apart: 7 -> 7, of which waited for: 2 -> 1; matrix products, arithmetic and copies ran while one was open for 0% -> 0% of each run, Pallas kernels for 32% -> 33%
where the time goes in v3:
time: 38.2 us; the launch traced here: 38.1 us
  Pallas kernels  19.3 us (51%)
  starting transfers between devices  16.1 us (42%)
  waiting for transfers between devices  2.04 us (5%)
  between operations  0.72 us (2%)
    pallas_call x4, Pallas kernels, attend(): pl.pallas_call(functools.partial(attend_kernel, shift, after), in_specs=i...  18 us
    ppermute x7, starting transfers between devices, sent(): return lax.ppermute(value, ('pipe', 'tensor'), pairs)  16.1 us
    ppermute x7, waiting for transfers between devices, sent(): return lax.ppermute(value, ('pipe', 'tensor'), pairs)  2.04 us
    pallas_call x1, Pallas kernels, join_last(): pl.pallas_call(join_last_kernel, in_specs=[pl.BlockSpec(memory_space=pltp...  0.79 us
  transfers between devices with their start and end apart: 7, of which 1 were waited for; matrix products, arithmetic and copies ran while one was open for 0% of the time, Pallas kernels for 33%

profile of v3, /device:TPU:1, one launch (start us, length us, event | category | flops | bytes accessed | tf_op | source)
XLA Modules:
  0.0 38.1 jit_solution(13091582113239439228)
XLA Ops:
  0.7 5.6 %attend.4 = (bf16[4,144,256]{2,1,0:T(8,128)(2,1)S(1)}, s32[8,128]{1,0:T(8,128)S(1)}, bf16[34,4096]{1,0:T(8,128)(2,1)S(1)}, bf16[3,2048,256]{2,1,0:T(8,128)(2,1)S(1)}, bf16[3,2048,256]{2,1,0:T(8,128)(2,1)S(1)}) custom-call(s32[1]{0:T(128)S(6)} %copy.6.refs_0_, s32[1,2]{1,0:T(1,128)} %refs_1_.1, bf16[34,16384]{1,0:T(8,128)(2,1)} %bitcast.10, ...), custom_call_target="tpu_custom_call" | custom-call | flops 1140850688 | bytes 6291456 | tf_op jit(solution)/shard_map/attend/pallas_call | solution.py:293
  6.2 4.5 %collective-permute-start = (bf16[4,144,256]{2,1,0:T(8,128)(2,1)S(1)}, bf16[4,144,256]{2,1,0:T(8,128)(2,1)S(1)}, u32[]{:S(2)}, u32[]{:S(2)}) collective-permute-start(bf16[4,144,256]{2,1,0:T(8,128)(2,1)S(1)} %get-tuple-element.22), channel_id=1, source_target_pairs={{0,8},{1,9},{2,10},{3,11},{4,12},{5,13},{6,14},{7,15},{8,0},{9,1},... | collective-permute-start | bytes 884744 | tf_op jit(solution)/shard_map/ppermute | solution.py:398
  10.8 4.2 %attend.5 = (bf16[4,144,256]{2,1,0:T(8,128)(2,1)S(1)}, bf16[34,4096]{1,0:T(8,128)(2,1)S(1)}, bf16[3,2048,256]{2,1,0:T(8,128)(2,1)S(1)}, bf16[3,2048,256]{2,1,0:T(8,128)(2,1)S(1)}) custom-call(s32[1]{0:T(128)S(6)} %copy.6.refs_0_, s32[8,128]{1,0:T(8,128)S(1)} %get-tuple-element.23.refs_1_, bf16[34,4096]{1,0:T(8,128)(2,1)S(1)} %get-tuple-element.24.refs_2_, ...), custom_call_target="tpu_custom_call" | custom-call | flops 1140850688 | bytes 6291456 | tf_op jit(solution)/shard_map/attend/pallas_call | solution.py:293
  14.9 0.8 %collective-permute-start.1 = (bf16[4,144,256]{2,1,0:T(8,128)(2,1)S(1)}, bf16[4,144,256]{2,1,0:T(8,128)(2,1)S(1)}, u32[]{:S(2)}, u32[]{:S(2)}) collective-permute-start(bf16[4,144,256]{2,1,0:T(8,128)(2,1)S(1)} %get-tuple-element.27), channel_id=1, source_target_pairs={{0,12},{1,13},{2,14},{3,15},{4,0},{5,1},{6,2},{7,3},{8,4},{9,5},{1... | collective-permute-start | bytes 884744 | tf_op jit(solution)/shard_map/ppermute | solution.py:398
  15.7 4.2 %attend.6 = (bf16[4,144,256]{2,1,0:T(8,128)(2,1)S(1)}, bf16[34,4096]{1,0:T(8,128)(2,1)S(1)}, bf16[3,2048,256]{2,1,0:T(8,128)(2,1)S(1)}, bf16[3,2048,256]{2,1,0:T(8,128)(2,1)S(1)}) custom-call(s32[1]{0:T(128)S(6)} %copy.6.refs_0_, s32[8,128]{1,0:T(8,128)S(1)} %get-tuple-element.23.refs_1_, bf16[34,4096]{1,0:T(8,128)(2,1)S(1)} %get-tuple-element.28.refs_2_, ...), custom_call_target="tpu_custom_call" | custom-call | flops 1140850688 | bytes 6291456 | tf_op jit(solution)/shard_map/attend/pallas_call | solution.py:293
  19.9 2.2 %collective-permute-start.2 = (bf16[4,144,256]{2,1,0:T(8,128)(2,1)S(1)}, bf16[4,144,256]{2,1,0:T(8,128)(2,1)S(1)}, u32[]{:S(2)}, u32[]{:S(2)}) collective-permute-start(bf16[4,144,256]{2,1,0:T(8,128)(2,1)S(1)} %get-tuple-element.31), channel_id=1, source_target_pairs={{0,4},{1,5},{2,6},{3,7},{4,8},{5,9},{6,10},{7,11},{8,12},{9,13},{1... | collective-permute-start | bytes 884744 | tf_op jit(solution)/shard_map/ppermute | solution.py:398
  22.1 4.1 %attend.7.refs_3_ = bf16[4,144,256]{2,1,0:T(8,128)(2,1)S(1)} custom-call(s32[1]{0:T(128)S(6)} %copy.6.refs_0_, s32[8,128]{1,0:T(8,128)S(1)} %get-tuple-element.23.refs_1_, bf16[34,4096]{1,0:T(8,128)(2,1)S(1)} %get-tuple-element.32.refs_2_, bf16[3,2048,256]{2,1,0:T(8,128)(2,1)S(1)} %get-tuple-element.33.refs_3_, ...), custom_call_target="tpu_custom_call" | custom-call | flops 1140850688 | bytes 6291456 | tf_op jit(solution)/shard_map/attend/pallas_call | solution.py:293
  26.2 0.0 collective-permute-done.refs_0_
  26.2 0.0 collective-permute-done.1.refs_1_
  26.3 0.0 collective-permute-done.2.refs_2_
  26.3 0.5 %join_some.1 = (bf16[144,256]{1,0:T(8,128)(2,1)S(1)}, bf16[144,256]{1,0:T(8,128)(2,1)S(1)}, bf16[144,256]{1,0:T(8,128)(2,1)S(1)}, bf16[144,256]{1,0:T(8,128)(2,1)S(1)}) custom-call(bf16[4,144,256]{2,1,0:T(8,128)(2,1)S(1)} %collective-permute-done.refs_0_, bf16[4,144,256]{2,1,0:T(8,128)(2,1)S(1)} %collective-permute-done.1.refs_1_, ...), custom_call_target="tpu_custom_call" | custom-call | tf_op jit(solution)/shard_map/join_some/pallas_call | solution.py:355
  26.7 5.6 %collective-permute-start.3 = (bf16[144,256]{1,0:T(8,128)(2,1)S(1)}, bf16[144,256]{1,0:T(8,128)(2,1)S(1)}, u32[]{:S(2)}, u32[]{:S(2)}) collective-permute-start(bf16[144,256]{1,0:T(8,128)(2,1)S(1)} %get-tuple-element.35), channel_id=1, source_target_pairs={{0,18},{1,19},{2,16},{3,17},{4,22},{5,23},{6,20},{7,21},{8,26},{9,... | collective-permute-start | bytes 221192 | tf_op jit(solution)/shard_map/ppermute | solution.py:398
  32.3 0.0 collective-permute-start.4
  32.3 3.0 %collective-permute-start.5 = (bf16[144,256]{1,0:T(8,128)(2,1)S(1)}, bf16[144,256]{1,0:T(8,128)(2,1)S(1)}, u32[]{:S(2)}, u32[]{:S(2)}) collective-permute-start(bf16[144,256]{1,0:T(8,128)(2,1)S(1)} %get-tuple-element.37), channel_id=1, source_target_pairs={{0,19},{1,16},{2,17},{3,18},{4,23},{5,20},{6,21},{7,22},{8,27},{9,... | collective-permute-start | bytes 221192 | tf_op jit(solution)/shard_map/ppermute | solution.py:398
  35.3 0.0 collective-permute-start.6
  35.3 0.0 collective-permute-done.3.refs_0_
  35.3 2.0 %collective-permute-done.4.refs_1_ = bf16[144,256]{1,0:T(8,128)(2,1)S(1)} collective-permute-done((bf16[144,256]{1,0:T(8,128)(2,1)S(1)}, bf16[144,256]{1,0:T(8,128)(2,1)S(1)}, u32[]{:S(2)}, u32[]{:S(2)}) %collective-permute-start.4) | collective-permute-done | bytes 73760 | tf_op jit(solution)/shard_map/ppermute | solution.py:398
  37.3 0.0 collective-permute-done.5.refs_2_
  37.3 0.0 collective-permute-done.6.refs_3_
  37.3 0.8 %join_last.1 = bf16[34,1024]{1,0:T(8,128)(2,1)} custom-call(bf16[144,256]{1,0:T(8,128)(2,1)S(1)} %collective-permute-done.3.refs_0_, bf16[144,256]{1,0:T(8,128)(2,1)S(1)} %collective-permute-done.4.refs_1_, bf16[144,256]{1,0:T(8,128)(2,1)S(1)} %collective-permute-done.5.refs_2_, bf16[144,256]{1,0:T(8,128)(2,1)S(1)} %collective-permute-done.6.refs_3_), custom_call_target="tpu_custom_call" | custom-call | tf_op jit(solution)/shard_map/join_last/pallas_call | solution.py:377
Async XLA Ops:
  6.2 20.0 %collective-permute-start = (bf16[4,144,256]{2,1,0:T(8,128)(2,1)S(1)}, bf16[4,144,256]{2,1,0:T(8,128)(2,1)S(1)}, u32[]{:S(2)}, u32[]{:S(2)}) collective-permute-start(bf16[4,144,256]{2,1,0:T(8,128)(2,1)S(1)} %get-tuple-element.22), channel_id=1, source_target_pairs={{0,8},{1,9},{2,10},{3,11},{4,12},{5,13},{6,14},{7,15},{8,0},{9,1},... | collective-permute-start | bytes 884744 | tf_op jit(solution)/shard_map/ppermute | solution.py:398
  14.9 11.3 %collective-permute-start.1 = (bf16[4,144,256]{2,1,0:T(8,128)(2,1)S(1)}, bf16[4,144,256]{2,1,0:T(8,128)(2,1)S(1)}, u32[]{:S(2)}, u32[]{:S(2)}) collective-permute-start(bf16[4,144,256]{2,1,0:T(8,128)(2,1)S(1)} %get-tuple-element.27), channel_id=1, source_target_pairs={{0,12},{1,13},{2,14},{3,15},{4,0},{5,1},{6,2},{7,3},{8,4},{9,5},{1... | collective-permute-start | bytes 884744 | tf_op jit(solution)/shard_map/ppermute | solution.py:398
  19.9 6.4 %collective-permute-start.2 = (bf16[4,144,256]{2,1,0:T(8,128)(2,1)S(1)}, bf16[4,144,256]{2,1,0:T(8,128)(2,1)S(1)}, u32[]{:S(2)}, u32[]{:S(2)}) collective-permute-start(bf16[4,144,256]{2,1,0:T(8,128)(2,1)S(1)} %get-tuple-element.31), channel_id=1, source_target_pairs={{0,4},{1,5},{2,6},{3,7},{4,8},{5,9},{6,10},{7,11},{8,12},{9,13},{1... | collective-permute-start | bytes 884744 | tf_op jit(solution)/shard_map/ppermute | solution.py:398
  26.7 8.6 %collective-permute-start.3 = (bf16[144,256]{1,0:T(8,128)(2,1)S(1)}, bf16[144,256]{1,0:T(8,128)(2,1)S(1)}, u32[]{:S(2)}, u32[]{:S(2)}) collective-permute-start(bf16[144,256]{1,0:T(8,128)(2,1)S(1)} %get-tuple-element.35), channel_id=1, source_target_pairs={{0,18},{1,19},{2,16},{3,17},{4,22},{5,23},{6,20},{7,21},{8,26},{9,... | collective-permute-start | bytes 221192 | tf_op jit(solution)/shard_map/ppermute | solution.py:398
  32.3 5.0 %collective-permute-start.4 = (bf16[144,256]{1,0:T(8,128)(2,1)S(1)}, bf16[144,256]{1,0:T(8,128)(2,1)S(1)}, u32[]{:S(2)}, u32[]{:S(2)}) collective-permute-start(bf16[144,256]{1,0:T(8,128)(2,1)S(1)} %get-tuple-element.36), channel_id=1, source_target_pairs={{0,17},{1,18},{2,19},{3,16},{4,21},{5,22},{6,23},{7,20},{8,25},{9,... | collective-permute-start | bytes 221192 | tf_op jit(solution)/shard_map/ppermute | solution.py:398
  32.3 5.0 %collective-permute-start.5 = (bf16[144,256]{1,0:T(8,128)(2,1)S(1)}, bf16[144,256]{1,0:T(8,128)(2,1)S(1)}, u32[]{:S(2)}, u32[]{:S(2)}) collective-permute-start(bf16[144,256]{1,0:T(8,128)(2,1)S(1)} %get-tuple-element.37), channel_id=1, source_target_pairs={{0,19},{1,16},{2,17},{3,18},{4,23},{5,20},{6,21},{7,22},{8,27},{9,... | collective-permute-start | bytes 221192 | tf_op jit(solution)/shard_map/ppermute | solution.py:398
  35.3 2.0 %collective-permute-start.6 = (bf16[144,256]{1,0:T(8,128)(2,1)S(1)}, bf16[144,256]{1,0:T(8,128)(2,1)S(1)}, u32[]{:S(2)}, u32[]{:S(2)}) collective-permute-start(bf16[144,256]{1,0:T(8,128)(2,1)S(1)} %get-tuple-element.38), channel_id=1, source_target_pairs={{0,16},{1,17},{2,18},{3,19},{4,20},{5,21},{6,22},{7,23},{8,24},{9,... | collective-permute-start | bytes 221192 | tf_op jit(solution)/shard_map/ppermute | solution.py:398

commit v4 on v3

--- a/solution.py
+++ b/solution.py
@@ -25,8 +25,8 @@
 DEAD = -1e30
 FLOOR = -1e29
 VMEM_LIMIT = 36 * 1024 * 1024
-FETCHED = ("q", "k", "n", "v", "k0", "v0", "k1", "v1")
-FIRST_SCHEDULE = "A0A1AA" "xBa0Ba0B0B" "Wb01b01" "111"
+FETCHED = ("q", "k", "K", "n", "v", "k0", "v0", "k1", "v1")
+FIRST_SCHEDULE = "A0A1AA" "xBBa0Ba0B0" "Wb01b01" "111"
 SCHEDULE = "A0A1AA" "Ba0Ba0B0B" "b01b01" "111"
 
 
@@ -110,7 +110,7 @@
     return lax.rem(here + by, ACROSS)
 
 
-def fetches(shift, sources, targets, sems):
+def fetches(shift, sources, targets, sems, by_head=False):
     section, slow, _ = place_of_device()
     pair = moved(slow, jnp.where(section == 0, shift[0], shift[1]))
     q_hbm, k_hbm, v_hbm = sources
@@ -123,6 +123,10 @@
     for name, sequence in (("", DEC), *((str(b), b) for b in range(DEC))):
         for kind, hbm, ref in (("k", k_hbm, k_ref), ("v", v_hbm, v_ref)):
             moves[kind + name] = (hbm.at[sequence, :, columns(PAIR * HD)], ref.at[sequence])
+    if by_head:
+        for n, name in enumerate(("k", "K")):
+            head = pl.ds(pl.multiple_of((pair * PAIR + n) * HD, HD), HD)
+            moves[name] = (k_hbm.at[DEC, :, head], k_ref.at[DEC, :, n * HD : (n + 1) * HD])
     return {
         name: pltpu.make_async_copy(*move, sems.at[n]) for n, (name, move) in enumerate(moves.items())
     }
@@ -155,7 +159,7 @@
 
     waiting = {}
     if first:
-        waiting = fetches(shift, sources, held, sems)
+        waiting = fetches(shift, sources, held, sems, True)
         waiting["n"] = pltpu.make_async_copy(lengths_hbm, lengths, sems.at[len(waiting)])
         for name in FETCHED:
             waiting[name].start()
@@ -215,7 +219,7 @@
             streams[str(b)] = decode_of(b, rows, k_ref, v_ref, length - offset)
         for name in FIRST_SCHEDULE if first else SCHEDULE:
             if name == "x":
-                wait(("v", "k0"))
+                wait(("K", "v", "k0"))
             elif name == "W":
                 wait(list(waiting))
             else:
@@ -284,8 +288,8 @@
     scratch = [
         pltpu.VMEM((local_len, LANES), jnp.float32),
         pltpu.VMEM((local_len, LANES), jnp.float32),
-        pltpu.SemaphoreType.DMA((2 * sequences + 2,)),
-        pltpu.SemaphoreType.DMA((2 * sequences + 2,)),
+        pltpu.SemaphoreType.DMA((2 * sequences + 3,)),
+        pltpu.SemaphoreType.DMA((2 * sequences + 3,)),
     ]
     if first:
         scratch.append(pltpu.SMEM(lengths.shape, jnp.int32))

time: 38.2 us -> 38.1 us (level)
  no operation moved by 1% of the time
where the time goes in v4:
time: 38.1 us; the launch traced here: 38 us
  Pallas kernels  19.2 us (50%)
  starting transfers between devices  16.1 us (42%)
  waiting for transfers between devices  2.04 us (5%)
  between operations  0.72 us (2%)
    pallas_call x4, Pallas kernels, attend(): pl.pallas_call(functools.partial(attend_kernel, shift, after), in_specs=i...  18 us
    ppermute x7, starting transfers between devices, sent(): return lax.ppermute(value, ('pipe', 'tensor'), pairs)  16.1 us
    ppermute x7, waiting for transfers between devices, sent(): return lax.ppermute(value, ('pipe', 'tensor'), pairs)  2.04 us
    pallas_call x1, Pallas kernels, join_last(): pl.pallas_call(join_last_kernel, in_specs=[pl.BlockSpec(memory_space=pltp...  0.79 us
  transfers between devices with their start and end apart: 7, of which 1 were waited for; matrix products, arithmetic and copies ran while one was open for 0% of the time, Pallas kernels for 33%

profile of v4, /device:TPU:1, one launch (start us, length us, event | category | flops | bytes accessed | tf_op | source)
XLA Modules:
  0.0 38.0 jit_solution(5312258590201472672)
XLA Ops:
  0.7 5.4 %attend.4 = (bf16[4,144,256]{2,1,0:T(8,128)(2,1)S(1)}, s32[8,128]{1,0:T(8,128)S(1)}, bf16[34,4096]{1,0:T(8,128)(2,1)S(1)}, bf16[3,2048,256]{2,1,0:T(8,128)(2,1)S(1)}, bf16[3,2048,256]{2,1,0:T(8,128)(2,1)S(1)}) custom-call(s32[1]{0:T(128)S(6)} %copy.6.refs_0_, s32[1,2]{1,0:T(1,128)} %refs_1_.1, bf16[34,16384]{1,0:T(8,128)(2,1)} %bitcast.10, ...), custom_call_target="tpu_custom_call" | custom-call | flops 1140850688 | bytes 6291456 | tf_op jit(solution)/shard_map/attend/pallas_call | solution.py:297
  6.1 4.5 %collective-permute-start = (bf16[4,144,256]{2,1,0:T(8,128)(2,1)S(1)}, bf16[4,144,256]{2,1,0:T(8,128)(2,1)S(1)}, u32[]{:S(2)}, u32[]{:S(2)}) collective-permute-start(bf16[4,144,256]{2,1,0:T(8,128)(2,1)S(1)} %get-tuple-element.22), channel_id=1, source_target_pairs={{0,8},{1,9},{2,10},{3,11},{4,12},{5,13},{6,14},{7,15},{8,0},{9,1},... | collective-permute-start | bytes 884744 | tf_op jit(solution)/shard_map/ppermute | solution.py:402
  10.6 4.2 %attend.5 = (bf16[4,144,256]{2,1,0:T(8,128)(2,1)S(1)}, bf16[34,4096]{1,0:T(8,128)(2,1)S(1)}, bf16[3,2048,256]{2,1,0:T(8,128)(2,1)S(1)}, bf16[3,2048,256]{2,1,0:T(8,128)(2,1)S(1)}) custom-call(s32[1]{0:T(128)S(6)} %copy.6.refs_0_, s32[8,128]{1,0:T(8,128)S(1)} %get-tuple-element.23.refs_1_, bf16[34,4096]{1,0:T(8,128)(2,1)S(1)} %get-tuple-element.24.refs_2_, ...), custom_call_target="tpu_custom_call" | custom-call | flops 1140850688 | bytes 6291456 | tf_op jit(solution)/shard_map/attend/pallas_call | solution.py:297
  14.8 0.8 %collective-permute-start.1 = (bf16[4,144,256]{2,1,0:T(8,128)(2,1)S(1)}, bf16[4,144,256]{2,1,0:T(8,128)(2,1)S(1)}, u32[]{:S(2)}, u32[]{:S(2)}) collective-permute-start(bf16[4,144,256]{2,1,0:T(8,128)(2,1)S(1)} %get-tuple-element.27), channel_id=1, source_target_pairs={{0,12},{1,13},{2,14},{3,15},{4,0},{5,1},{6,2},{7,3},{8,4},{9,5},{1... | collective-permute-start | bytes 884744 | tf_op jit(solution)/shard_map/ppermute | solution.py:402
  15.6 4.2 %attend.6 = (bf16[4,144,256]{2,1,0:T(8,128)(2,1)S(1)}, bf16[34,4096]{1,0:T(8,128)(2,1)S(1)}, bf16[3,2048,256]{2,1,0:T(8,128)(2,1)S(1)}, bf16[3,2048,256]{2,1,0:T(8,128)(2,1)S(1)}) custom-call(s32[1]{0:T(128)S(6)} %copy.6.refs_0_, s32[8,128]{1,0:T(8,128)S(1)} %get-tuple-element.23.refs_1_, bf16[34,4096]{1,0:T(8,128)(2,1)S(1)} %get-tuple-element.28.refs_2_, ...), custom_call_target="tpu_custom_call" | custom-call | flops 1140850688 | bytes 6291456 | tf_op jit(solution)/shard_map/attend/pallas_call | solution.py:297
  19.8 2.2 %collective-permute-start.2 = (bf16[4,144,256]{2,1,0:T(8,128)(2,1)S(1)}, bf16[4,144,256]{2,1,0:T(8,128)(2,1)S(1)}, u32[]{:S(2)}, u32[]{:S(2)}) collective-permute-start(bf16[4,144,256]{2,1,0:T(8,128)(2,1)S(1)} %get-tuple-element.31), channel_id=1, source_target_pairs={{0,4},{1,5},{2,6},{3,7},{4,8},{5,9},{6,10},{7,11},{8,12},{9,13},{1... | collective-permute-start | bytes 884744 | tf_op jit(solution)/shard_map/ppermute | solution.py:402
  22.0 4.2 %attend.7.refs_3_ = bf16[4,144,256]{2,1,0:T(8,128)(2,1)S(1)} custom-call(s32[1]{0:T(128)S(6)} %copy.6.refs_0_, s32[8,128]{1,0:T(8,128)S(1)} %get-tuple-element.23.refs_1_, bf16[34,4096]{1,0:T(8,128)(2,1)S(1)} %get-tuple-element.32.refs_2_, bf16[3,2048,256]{2,1,0:T(8,128)(2,1)S(1)} %get-tuple-element.33.refs_3_, ...), custom_call_target="tpu_custom_call" | custom-call | flops 1140850688 | bytes 6291456 | tf_op jit(solution)/shard_map/attend/pallas_call | solution.py:297
  26.2 0.0 collective-permute-done.refs_0_
  26.2 0.0 collective-permute-done.1.refs_1_
  26.2 0.0 collective-permute-done.2.refs_2_
  26.2 0.5 %join_some.1 = (bf16[144,256]{1,0:T(8,128)(2,1)S(1)}, bf16[144,256]{1,0:T(8,128)(2,1)S(1)}, bf16[144,256]{1,0:T(8,128)(2,1)S(1)}, bf16[144,256]{1,0:T(8,128)(2,1)S(1)}) custom-call(bf16[4,144,256]{2,1,0:T(8,128)(2,1)S(1)} %collective-permute-done.refs_0_, bf16[4,144,256]{2,1,0:T(8,128)(2,1)S(1)} %collective-permute-done.1.refs_1_, ...), custom_call_target="tpu_custom_call" | custom-call | tf_op jit(solution)/shard_map/join_some/pallas_call | solution.py:359
  26.6 5.6 %collective-permute-start.3 = (bf16[144,256]{1,0:T(8,128)(2,1)S(1)}, bf16[144,256]{1,0:T(8,128)(2,1)S(1)}, u32[]{:S(2)}, u32[]{:S(2)}) collective-permute-start(bf16[144,256]{1,0:T(8,128)(2,1)S(1)} %get-tuple-element.35), channel_id=1, source_target_pairs={{0,18},{1,19},{2,16},{3,17},{4,22},{5,23},{6,20},{7,21},{8,26},{9,... | collective-permute-start | bytes 221192 | tf_op jit(solution)/shard_map/ppermute | solution.py:402
  32.2 0.0 collective-permute-start.4
  32.3 3.0 %collective-permute-start.5 = (bf16[144,256]{1,0:T(8,128)(2,1)S(1)}, bf16[144,256]{1,0:T(8,128)(2,1)S(1)}, u32[]{:S(2)}, u32[]{:S(2)}) collective-permute-start(bf16[144,256]{1,0:T(8,128)(2,1)S(1)} %get-tuple-element.37), channel_id=1, source_target_pairs={{0,19},{1,16},{2,17},{3,18},{4,23},{5,20},{6,21},{7,22},{8,27},{9,... | collective-permute-start | bytes 221192 | tf_op jit(solution)/shard_map/ppermute | solution.py:402
  35.2 0.0 collective-permute-start.6
  35.2 0.0 collective-permute-done.3.refs_0_
  35.2 2.0 %collective-permute-done.4.refs_1_ = bf16[144,256]{1,0:T(8,128)(2,1)S(1)} collective-permute-done((bf16[144,256]{1,0:T(8,128)(2,1)S(1)}, bf16[144,256]{1,0:T(8,128)(2,1)S(1)}, u32[]{:S(2)}, u32[]{:S(2)}) %collective-permute-start.4) | collective-permute-done | bytes 73760 | tf_op jit(solution)/shard_map/ppermute | solution.py:402
  37.2 0.0 collective-permute-done.5.refs_2_
  37.2 0.0 collective-permute-done.6.refs_3_
  37.2 0.8 %join_last.1 = bf16[34,1024]{1,0:T(8,128)(2,1)} custom-call(bf16[144,256]{1,0:T(8,128)(2,1)S(1)} %collective-permute-done.3.refs_0_, bf16[144,256]{1,0:T(8,128)(2,1)S(1)} %collective-permute-done.4.refs_1_, bf16[144,256]{1,0:T(8,128)(2,1)S(1)} %collective-permute-done.5.refs_2_, bf16[144,256]{1,0:T(8,128)(2,1)S(1)} %collective-permute-done.6.refs_3_), custom_call_target="tpu_custom_call" | custom-call | tf_op jit(solution)/shard_map/join_last/pallas_call | solution.py:381
Async XLA Ops:
  6.1 20.1 %collective-permute-start = (bf16[4,144,256]{2,1,0:T(8,128)(2,1)S(1)}, bf16[4,144,256]{2,1,0:T(8,128)(2,1)S(1)}, u32[]{:S(2)}, u32[]{:S(2)}) collective-permute-start(bf16[4,144,256]{2,1,0:T(8,128)(2,1)S(1)} %get-tuple-element.22), channel_id=1, source_target_pairs={{0,8},{1,9},{2,10},{3,11},{4,12},{5,13},{6,14},{7,15},{8,0},{9,1},... | collective-permute-start | bytes 884744 | tf_op jit(solution)/shard_map/ppermute | solution.py:402
  14.8 11.4 %collective-permute-start.1 = (bf16[4,144,256]{2,1,0:T(8,128)(2,1)S(1)}, bf16[4,144,256]{2,1,0:T(8,128)(2,1)S(1)}, u32[]{:S(2)}, u32[]{:S(2)}) collective-permute-start(bf16[4,144,256]{2,1,0:T(8,128)(2,1)S(1)} %get-tuple-element.27), channel_id=1, source_target_pairs={{0,12},{1,13},{2,14},{3,15},{4,0},{5,1},{6,2},{7,3},{8,4},{9,5},{1... | collective-permute-start | bytes 884744 | tf_op jit(solution)/shard_map/ppermute | solution.py:402
  19.8 6.4 %collective-permute-start.2 = (bf16[4,144,256]{2,1,0:T(8,128)(2,1)S(1)}, bf16[4,144,256]{2,1,0:T(8,128)(2,1)S(1)}, u32[]{:S(2)}, u32[]{:S(2)}) collective-permute-start(bf16[4,144,256]{2,1,0:T(8,128)(2,1)S(1)} %get-tuple-element.31), channel_id=1, source_target_pairs={{0,4},{1,5},{2,6},{3,7},{4,8},{5,9},{6,10},{7,11},{8,12},{9,13},{1... | collective-permute-start | bytes 884744 | tf_op jit(solution)/shard_map/ppermute | solution.py:402
  26.6 8.6 %collective-permute-start.3 = (bf16[144,256]{1,0:T(8,128)(2,1)S(1)}, bf16[144,256]{1,0:T(8,128)(2,1)S(1)}, u32[]{:S(2)}, u32[]{:S(2)}) collective-permute-start(bf16[144,256]{1,0:T(8,128)(2,1)S(1)} %get-tuple-element.35), channel_id=1, source_target_pairs={{0,18},{1,19},{2,16},{3,17},{4,22},{5,23},{6,20},{7,21},{8,26},{9,... | collective-permute-start | bytes 221192 | tf_op jit(solution)/shard_map/ppermute | solution.py:402
  32.2 5.0 %collective-permute-start.4 = (bf16[144,256]{1,0:T(8,128)(2,1)S(1)}, bf16[144,256]{1,0:T(8,128)(2,1)S(1)}, u32[]{:S(2)}, u32[]{:S(2)}) collective-permute-start(bf16[144,256]{1,0:T(8,128)(2,1)S(1)} %get-tuple-element.36), channel_id=1, source_target_pairs={{0,17},{1,18},{2,19},{3,16},{4,21},{5,22},{6,23},{7,20},{8,25},{9,... | collective-permute-start | bytes 221192 | tf_op jit(solution)/shard_map/ppermute | solution.py:402
  32.3 5.0 %collective-permute-start.5 = (bf16[144,256]{1,0:T(8,128)(2,1)S(1)}, bf16[144,256]{1,0:T(8,128)(2,1)S(1)}, u32[]{:S(2)}, u32[]{:S(2)}) collective-permute-start(bf16[144,256]{1,0:T(8,128)(2,1)S(1)} %get-tuple-element.37), channel_id=1, source_target_pairs={{0,19},{1,16},{2,17},{3,18},{4,23},{5,20},{6,21},{7,22},{8,27},{9,... | collective-permute-start | bytes 221192 | tf_op jit(solution)/shard_map/ppermute | solution.py:402
  35.2 2.0 %collective-permute-start.6 = (bf16[144,256]{1,0:T(8,128)(2,1)S(1)}, bf16[144,256]{1,0:T(8,128)(2,1)S(1)}, u32[]{:S(2)}, u32[]{:S(2)}) collective-permute-start(bf16[144,256]{1,0:T(8,128)(2,1)S(1)} %get-tuple-element.38), channel_id=1, source_target_pairs={{0,16},{1,17},{2,18},{3,19},{4,20},{5,21},{6,22},{7,23},{8,24},{9,... | collective-permute-start | bytes 221192 | tf_op jit(solution)/shard_map/ppermute | solution.py:402

commit v5 on v4

--- a/solution.py
+++ b/solution.py
@@ -368,10 +368,10 @@
 
 def join_last_kernel(*refs):
     (acc, _, total), dec = joined(refs[:-1])
-    result = (acc / total).T
+    result = (acc * (1.0 / total)).T
     rows = []
     for dec_acc, _, dec_total in dec:
-        one = dec_acc / dec_total
+        one = dec_acc * (1.0 / dec_total)
         rows.append(jnp.concatenate([one[g : g + 1] for g in range(HALF)], 1))
     rows.append(jnp.concatenate([result[g * PRE : (g + 1) * PRE] for g in range(HALF)], 1))
     refs[-1][...] = jnp.concatenate(rows, 0).astype(jnp.bfloat16)

time: 38.1 us -> 38.1 us (level)
  no operation moved by 1% of the time
where the time goes in v5:
time: 38.1 us; the launch traced here: 38 us
  Pallas kernels  19.2 us (50%)
  starting transfers between devices  16.1 us (42%)
  waiting for transfers between devices  2.04 us (5%)
  between operations  0.72 us (2%)
    pallas_call x4, Pallas kernels, attend(): pl.pallas_call(functools.partial(attend_kernel, shift, after), in_specs=i...  18 us
    ppermute x7, starting transfers between devices, sent(): return lax.ppermute(value, ('pipe', 'tensor'), pairs)  16.1 us
    ppermute x7, waiting for transfers between devices, sent(): return lax.ppermute(value, ('pipe', 'tensor'), pairs)  2.04 us
    pallas_call x1, Pallas kernels, join_last(): pl.pallas_call(join_last_kernel, in_specs=[pl.BlockSpec(memory_space=pltp...  0.79 us
  transfers between devices with their start and end apart: 7, of which 1 were waited for; matrix products, arithmetic and copies ran while one was open for 0% of the time, Pallas kernels for 33%

profile of v5, /device:TPU:1, one launch (start us, length us, event | category | flops | bytes accessed | tf_op | source)
XLA Modules:
  0.0 38.0 jit_solution(3018543939920732079)
XLA Ops:
  0.7 5.4 %attend.4 = (bf16[4,144,256]{2,1,0:T(8,128)(2,1)S(1)}, s32[8,128]{1,0:T(8,128)S(1)}, bf16[34,4096]{1,0:T(8,128)(2,1)S(1)}, bf16[3,2048,256]{2,1,0:T(8,128)(2,1)S(1)}, bf16[3,2048,256]{2,1,0:T(8,128)(2,1)S(1)}) custom-call(s32[1]{0:T(128)S(6)} %copy.6.refs_0_, s32[1,2]{1,0:T(1,128)} %refs_1_.1, bf16[34,16384]{1,0:T(8,128)(2,1)} %bitcast.10, ...), custom_call_target="tpu_custom_call" | custom-call | flops 1140850688 | bytes 6291456 | tf_op jit(solution)/shard_map/attend/pallas_call | solution.py:297
  6.1 4.5 %collective-permute-start = (bf16[4,144,256]{2,1,0:T(8,128)(2,1)S(1)}, bf16[4,144,256]{2,1,0:T(8,128)(2,1)S(1)}, u32[]{:S(2)}, u32[]{:S(2)}) collective-permute-start(bf16[4,144,256]{2,1,0:T(8,128)(2,1)S(1)} %get-tuple-element.22), channel_id=1, source_target_pairs={{0,8},{1,9},{2,10},{3,11},{4,12},{5,13},{6,14},{7,15},{8,0},{9,1},... | collective-permute-start | bytes 884744 | tf_op jit(solution)/shard_map/ppermute | solution.py:402
  10.6 4.2 %attend.5 = (bf16[4,144,256]{2,1,0:T(8,128)(2,1)S(1)}, bf16[34,4096]{1,0:T(8,128)(2,1)S(1)}, bf16[3,2048,256]{2,1,0:T(8,128)(2,1)S(1)}, bf16[3,2048,256]{2,1,0:T(8,128)(2,1)S(1)}) custom-call(s32[1]{0:T(128)S(6)} %copy.6.refs_0_, s32[8,128]{1,0:T(8,128)S(1)} %get-tuple-element.23.refs_1_, bf16[34,4096]{1,0:T(8,128)(2,1)S(1)} %get-tuple-element.24.refs_2_, ...), custom_call_target="tpu_custom_call" | custom-call | flops 1140850688 | bytes 6291456 | tf_op jit(solution)/shard_map/attend/pallas_call | solution.py:297
  14.8 0.8 %collective-permute-start.1 = (bf16[4,144,256]{2,1,0:T(8,128)(2,1)S(1)}, bf16[4,144,256]{2,1,0:T(8,128)(2,1)S(1)}, u32[]{:S(2)}, u32[]{:S(2)}) collective-permute-start(bf16[4,144,256]{2,1,0:T(8,128)(2,1)S(1)} %get-tuple-element.27), channel_id=1, source_target_pairs={{0,12},{1,13},{2,14},{3,15},{4,0},{5,1},{6,2},{7,3},{8,4},{9,5},{1... | collective-permute-start | bytes 884744 | tf_op jit(solution)/shard_map/ppermute | solution.py:402
  15.6 4.2 %attend.6 = (bf16[4,144,256]{2,1,0:T(8,128)(2,1)S(1)}, bf16[34,4096]{1,0:T(8,128)(2,1)S(1)}, bf16[3,2048,256]{2,1,0:T(8,128)(2,1)S(1)}, bf16[3,2048,256]{2,1,0:T(8,128)(2,1)S(1)}) custom-call(s32[1]{0:T(128)S(6)} %copy.6.refs_0_, s32[8,128]{1,0:T(8,128)S(1)} %get-tuple-element.23.refs_1_, bf16[34,4096]{1,0:T(8,128)(2,1)S(1)} %get-tuple-element.28.refs_2_, ...), custom_call_target="tpu_custom_call" | custom-call | flops 1140850688 | bytes 6291456 | tf_op jit(solution)/shard_map/attend/pallas_call | solution.py:297
  19.8 2.2 %collective-permute-start.2 = (bf16[4,144,256]{2,1,0:T(8,128)(2,1)S(1)}, bf16[4,144,256]{2,1,0:T(8,128)(2,1)S(1)}, u32[]{:S(2)}, u32[]{:S(2)}) collective-permute-start(bf16[4,144,256]{2,1,0:T(8,128)(2,1)S(1)} %get-tuple-element.31), channel_id=1, source_target_pairs={{0,4},{1,5},{2,6},{3,7},{4,8},{5,9},{6,10},{7,11},{8,12},{9,13},{1... | collective-permute-start | bytes 884744 | tf_op jit(solution)/shard_map/ppermute | solution.py:402
  22.0 4.2 %attend.7.refs_3_ = bf16[4,144,256]{2,1,0:T(8,128)(2,1)S(1)} custom-call(s32[1]{0:T(128)S(6)} %copy.6.refs_0_, s32[8,128]{1,0:T(8,128)S(1)} %get-tuple-element.23.refs_1_, bf16[34,4096]{1,0:T(8,128)(2,1)S(1)} %get-tuple-element.32.refs_2_, bf16[3,2048,256]{2,1,0:T(8,128)(2,1)S(1)} %get-tuple-element.33.refs_3_, ...), custom_call_target="tpu_custom_call" | custom-call | flops 1140850688 | bytes 6291456 | tf_op jit(solution)/shard_map/attend/pallas_call | solution.py:297
  26.2 0.0 collective-permute-done.refs_0_
  26.2 0.0 collective-permute-done.1.refs_1_
  26.2 0.0 collective-permute-done.2.refs_2_
  26.2 0.5 %join_some.1 = (bf16[144,256]{1,0:T(8,128)(2,1)S(1)}, bf16[144,256]{1,0:T(8,128)(2,1)S(1)}, bf16[144,256]{1,0:T(8,128)(2,1)S(1)}, bf16[144,256]{1,0:T(8,128)(2,1)S(1)}) custom-call(bf16[4,144,256]{2,1,0:T(8,128)(2,1)S(1)} %collective-permute-done.refs_0_, bf16[4,144,256]{2,1,0:T(8,128)(2,1)S(1)} %collective-permute-done.1.refs_1_, ...), custom_call_target="tpu_custom_call" | custom-call | tf_op jit(solution)/shard_map/join_some/pallas_call | solution.py:359
  26.6 5.6 %collective-permute-start.3 = (bf16[144,256]{1,0:T(8,128)(2,1)S(1)}, bf16[144,256]{1,0:T(8,128)(2,1)S(1)}, u32[]{:S(2)}, u32[]{:S(2)}) collective-permute-start(bf16[144,256]{1,0:T(8,128)(2,1)S(1)} %get-tuple-element.35), channel_id=1, source_target_pairs={{0,18},{1,19},{2,16},{3,17},{4,22},{5,23},{6,20},{7,21},{8,26},{9,... | collective-permute-start | bytes 221192 | tf_op jit(solution)/shard_map/ppermute | solution.py:402
  32.2 0.0 collective-permute-start.4
  32.3 3.0 %collective-permute-start.5 = (bf16[144,256]{1,0:T(8,128)(2,1)S(1)}, bf16[144,256]{1,0:T(8,128)(2,1)S(1)}, u32[]{:S(2)}, u32[]{:S(2)}) collective-permute-start(bf16[144,256]{1,0:T(8,128)(2,1)S(1)} %get-tuple-element.37), channel_id=1, source_target_pairs={{0,19},{1,16},{2,17},{3,18},{4,23},{5,20},{6,21},{7,22},{8,27},{9,... | collective-permute-start | bytes 221192 | tf_op jit(solution)/shard_map/ppermute | solution.py:402
  35.2 0.0 collective-permute-start.6
  35.2 0.0 collective-permute-done.3.refs_0_
  35.2 2.0 %collective-permute-done.4.refs_1_ = bf16[144,256]{1,0:T(8,128)(2,1)S(1)} collective-permute-done((bf16[144,256]{1,0:T(8,128)(2,1)S(1)}, bf16[144,256]{1,0:T(8,128)(2,1)S(1)}, u32[]{:S(2)}, u32[]{:S(2)}) %collective-permute-start.4) | collective-permute-done | bytes 73760 | tf_op jit(solution)/shard_map/ppermute | solution.py:402
  37.2 0.0 collective-permute-done.5.refs_2_
  37.2 0.0 collective-permute-done.6.refs_3_
  37.2 0.8 %join_last.1 = bf16[34,1024]{1,0:T(8,128)(2,1)} custom-call(bf16[144,256]{1,0:T(8,128)(2,1)S(1)} %collective-permute-done.3.refs_0_, bf16[144,256]{1,0:T(8,128)(2,1)S(1)} %collective-permute-done.4.refs_1_, bf16[144,256]{1,0:T(8,128)(2,1)S(1)} %collective-permute-done.5.refs_2_, bf16[144,256]{1,0:T(8,128)(2,1)S(1)} %collective-permute-done.6.refs_3_), custom_call_target="tpu_custom_call" | custom-call | tf_op jit(solution)/shard_map/join_last/pallas_call | solution.py:381
Async XLA Ops:
  6.1 20.1 %collective-permute-start = (bf16[4,144,256]{2,1,0:T(8,128)(2,1)S(1)}, bf16[4,144,256]{2,1,0:T(8,128)(2,1)S(1)}, u32[]{:S(2)}, u32[]{:S(2)}) collective-permute-start(bf16[4,144,256]{2,1,0:T(8,128)(2,1)S(1)} %get-tuple-element.22), channel_id=1, source_target_pairs={{0,8},{1,9},{2,10},{3,11},{4,12},{5,13},{6,14},{7,15},{8,0},{9,1},... | collective-permute-start | bytes 884744 | tf_op jit(solution)/shard_map/ppermute | solution.py:402
  14.8 11.4 %collective-permute-start.1 = (bf16[4,144,256]{2,1,0:T(8,128)(2,1)S(1)}, bf16[4,144,256]{2,1,0:T(8,128)(2,1)S(1)}, u32[]{:S(2)}, u32[]{:S(2)}) collective-permute-start(bf16[4,144,256]{2,1,0:T(8,128)(2,1)S(1)} %get-tuple-element.27), channel_id=1, source_target_pairs={{0,12},{1,13},{2,14},{3,15},{4,0},{5,1},{6,2},{7,3},{8,4},{9,5},{1... | collective-permute-start | bytes 884744 | tf_op jit(solution)/shard_map/ppermute | solution.py:402
  19.8 6.4 %collective-permute-start.2 = (bf16[4,144,256]{2,1,0:T(8,128)(2,1)S(1)}, bf16[4,144,256]{2,1,0:T(8,128)(2,1)S(1)}, u32[]{:S(2)}, u32[]{:S(2)}) collective-permute-start(bf16[4,144,256]{2,1,0:T(8,128)(2,1)S(1)} %get-tuple-element.31), channel_id=1, source_target_pairs={{0,4},{1,5},{2,6},{3,7},{4,8},{5,9},{6,10},{7,11},{8,12},{9,13},{1... | collective-permute-start | bytes 884744 | tf_op jit(solution)/shard_map/ppermute | solution.py:402
  26.6 8.6 %collective-permute-start.3 = (bf16[144,256]{1,0:T(8,128)(2,1)S(1)}, bf16[144,256]{1,0:T(8,128)(2,1)S(1)}, u32[]{:S(2)}, u32[]{:S(2)}) collective-permute-start(bf16[144,256]{1,0:T(8,128)(2,1)S(1)} %get-tuple-element.35), channel_id=1, source_target_pairs={{0,18},{1,19},{2,16},{3,17},{4,22},{5,23},{6,20},{7,21},{8,26},{9,... | collective-permute-start | bytes 221192 | tf_op jit(solution)/shard_map/ppermute | solution.py:402
  32.2 5.0 %collective-permute-start.4 = (bf16[144,256]{1,0:T(8,128)(2,1)S(1)}, bf16[144,256]{1,0:T(8,128)(2,1)S(1)}, u32[]{:S(2)}, u32[]{:S(2)}) collective-permute-start(bf16[144,256]{1,0:T(8,128)(2,1)S(1)} %get-tuple-element.36), channel_id=1, source_target_pairs={{0,17},{1,18},{2,19},{3,16},{4,21},{5,22},{6,23},{7,20},{8,25},{9,... | collective-permute-start | bytes 221192 | tf_op jit(solution)/shard_map/ppermute | solution.py:402
  32.3 5.0 %collective-permute-start.5 = (bf16[144,256]{1,0:T(8,128)(2,1)S(1)}, bf16[144,256]{1,0:T(8,128)(2,1)S(1)}, u32[]{:S(2)}, u32[]{:S(2)}) collective-permute-start(bf16[144,256]{1,0:T(8,128)(2,1)S(1)} %get-tuple-element.37), channel_id=1, source_target_pairs={{0,19},{1,16},{2,17},{3,18},{4,23},{5,20},{6,21},{7,22},{8,27},{9,... | collective-permute-start | bytes 221192 | tf_op jit(solution)/shard_map/ppermute | solution.py:402
  35.2 2.0 %collective-permute-start.6 = (bf16[144,256]{1,0:T(8,128)(2,1)S(1)}, bf16[144,256]{1,0:T(8,128)(2,1)S(1)}, u32[]{:S(2)}, u32[]{:S(2)}) collective-permute-start(bf16[144,256]{1,0:T(8,128)(2,1)S(1)} %get-tuple-element.38), channel_id=1, source_target_pairs={{0,16},{1,17},{2,18},{3,19},{4,20},{5,21},{6,22},{7,23},{8,24},{9,... | collective-permute-start | bytes 221192 | tf_op jit(solution)/shard_map/ppermute | solution.py:402
